TPU v7x, 512 devices: a whole 4x4x16 slice. The times are simulated.
512 devices in a mesh: grp: 32 (over x, y, core), blk: 16 (over z).
Axes of the slice: x: 4, y: 4, z: 16, core: 2. Of those that a mesh axis runs over, the one named last changes fastest.
Arguments:
- dual_populace: float32 [19, 256, 256, 128], P(None, 'grp', 'blk'), may hold values from -6 to 6
- forward_motion_vector: float32 [3, 256, 256, 128], P(None, 'grp', 'blk'), may hold values from -0.4 to 0.4
- forward_heat_level: float32 [256, 256, 128], P('grp', 'blk'), may hold values from 0.5 to 1.5
- objective_heat_gradient: float32 [256, 256, 128], P('grp', 'blk'), may hold values from -6 to 6
- liquid_indicator: int32 [256, 256, 128], P('grp', 'blk'), may hold values 0 or 1
- filter_span_group: int32 [256, 256, 128], P('grp', 'blk'), may hold values from 0 to 3
Outputs:
- adjoint_out: float32 [19, 256, 256, 128], P(None, 'grp', 'blk')
- filtered: float32 [256, 256, 128], P('grp', 'blk')
All inputs are finite; a program needn't handle non-finite values. No bound on the sum of `liquid_indicator` on one device may be relied on, other than what follows from the above.
Results may differ from a plain program's by a relative error of at most 0.000031.
Values sent between devices are 32-bit elements; how exact they have to be, the bound alone decides.
A program may use at most 64 MiB of HBM per device.

v0:
```python
import jax
import jax.numpy as jnp
from jax import lax
from jax.sharding import PartitionSpec as P

STEPS = 3
SWEEPS = 8


VELOCITIES = (
    (0, 0, 0),
    (1, 0, 0),
    (-1, 0, 0),
    (0, 1, 0),
    (0, -1, 0),
    (0, 0, 1),
    (0, 0, -1),
    (1, 1, 0),
    (-1, -1, 0),
    (1, -1, 0),
    (-1, 1, 0),
    (1, 0, 1),
    (-1, 0, -1),
    (1, 0, -1),
    (-1, 0, 1),
    (0, 1, 1),
    (0, -1, -1),
    (0, 1, -1),
    (0, -1, 1),
)
WEIGHTS = (1.0 / 3.0,) + (1.0 / 18.0,) * 6 + (1.0 / 36.0,) * 12


def padded_2(x, sides, width):
    for axis, dim in sides:
        size, length = (lax.axis_size(axis), x.shape[dim])
        up = [(i, (i + 1) % size) for i in range(size - 1)]
        down = [(j, i) for i, j in up]
        last = lax.slice_in_dim(x, length - width, length, axis=dim)
        leading = lax.slice_in_dim(x, 0, width, axis=dim)
        before = lax.ppermute(last, axis, up)
        after = lax.ppermute(leading, axis, down)
        x = jnp.concatenate([before, x, after], axis=dim)
    return x


def collide(pulled, omega, vel_x, vel_y, vel_z, objective_heat_gradient):
    equilib = jnp.zeros_like(omega)
    average = jnp.zeros_like(omega)
    for population in range(19):
        cx, cy, cz = VELOCITIES[population]
        along = cx * vel_x + cy * vel_y + cz * vel_z
        equilib = equilib + WEIGHTS[population] * (1.0 + 3.0 * along) * pulled[population]
        average = average + WEIGHTS[population] * pulled[population]
    posts = [
        pulled[population]
        - omega * (pulled[population] - equilib)
        + WEIGHTS[population] * objective_heat_gradient
        for population in range(19)
    ]
    return (jnp.stack(posts), equilib - average)


def pull_from(extended):
    width_x, width_y, width_z = (extended.shape[1] - 2, extended.shape[2] - 2, extended.shape[3])
    padded = jnp.pad(extended, ((0, 0), (0, 0), (0, 0), (1, 1)))
    pieces = []
    for population in range(19):
        cx, cy, cz = VELOCITIES[population]
        pieces.append(
            padded[
                population,
                1 + cx : 1 + cx + width_x,
                1 + cy : 1 + cy + width_y,
                1 + cz : 1 + cz + width_z,
            ]
        )
    return jnp.stack(pieces)


def on_device(
    dual_populace,
    forward_motion_vector,
    forward_heat_level,
    objective_heat_gradient,
    liquid_indicator,
    filter_span_group,
):
    fluid = liquid_indicator.astype(jnp.float32)
    moving = forward_motion_vector * fluid[None]
    omega = 0.9 + 0.7 * fluid
    state = dual_populace
    gradient_map = jnp.zeros_like(forward_heat_level)
    for number in range(STEPS):
        extended = padded_2(state, (("grp", 1), ("blk", 2)), 1)
        pulled = pull_from(extended)
        state, correction_increment = collide(
            pulled, omega, moving[0], moving[1], moving[2], objective_heat_gradient
        )
        gradient_map = gradient_map + forward_heat_level * correction_increment
    radius_sq = 0.25 * jnp.power(4.0, filter_span_group.astype(jnp.float32))
    smooth = gradient_map
    denom = 1.0 + 6.0 * radius_sq
    for number in range(SWEEPS):
        rimmed = padded_2(smooth, (("grp", 0), ("blk", 1)), 1)
        padded = jnp.pad(rimmed, ((0, 0), (0, 0), (1, 1)))
        beside = padded[2:, 1:-1, 1:-1] + padded[:-2, 1:-1, 1:-1]
        beside = beside + padded[1:-1, 2:, 1:-1] + padded[1:-1, :-2, 1:-1]
        beside = beside + padded[1:-1, 1:-1, 2:] + padded[1:-1, 1:-1, :-2]
        smooth = (gradient_map + radius_sq * beside) / denom
    return (state, smooth)


def solution(mesh):
    in_specs = (
        P(None, "grp", "blk", None),
        P(None, "grp", "blk", None),
        P("grp", "blk", None),
        P("grp", "blk", None),
        P("grp", "blk", None),
        P("grp", "blk", None),
    )
    out_specs = (P(None, "grp", "blk", None), P("grp", "blk", None))
    return jax.shard_map(
        on_device, mesh=mesh, in_specs=in_specs, out_specs=out_specs, check_vma=False
    )
```

profile of v0, /device:TPU:6, one launch (start us, length us, event | category | flops | bytes accessed | tf_op | source)
XLA Modules:
  0.0 231.5 jit_solution(3235058283438377192)
XLA Ops:
  1.7 1.9 collective-permute-start.1
  3.6 5.8 %collective-permute-start = (f32[19,1,16,128]{3,2,1,0:T(8,128)S(1)}, f32[19,1,16,128]{3,2,1,0:T(8,128)S(1)}, u32[]{:S(2)}, u32[]{:S(2)}) collective-permute-start(f32[19,1,16,128]{3,2,1,0:T(8,128)S(1)} %get-tuple-element.61), channel_id=1, source_target_pairs={{16,0},{32,16},{48,32},{64,48},{80,64},{96,80},{112,96},{128,112},... | collective-permute-start | bytes 466952 | tf_op jit(solution)/shard_map/ppermute | solution.py:42
  12.2 3.8 %collective-permute-start.3 = (f32[19,10,1,128]{3,2,1,0:T(1,128)S(1)}, f32[19,10,1,128]{3,2,1,0:T(1,128)S(1)}, u32[]{:S(2)}, u32[]{:S(2)}) collective-permute-start(f32[19,10,1,128]{3,2,1,0:T(1,128)S(1)} %get-tuple-element.55), channel_id=1, source_target_pairs={{0,1},{1,2},{2,3},{3,4},{4,5},{5,6},{6,7},{7,8},{8,9},{9,10},{10,1... | collective-permute-start | bytes 291848 | tf_op jit(solution)/shard_map/ppermute | solution.py:41
  18.2 4.3 %collective-permute-done.2 = f32[19,10,1,128]{3,2,1,0:T(1,128)S(1)} collective-permute-done((f32[19,10,1,128]{3,2,1,0:T(1,128)S(1)}, f32[19,10,1,128]{3,2,1,0:T(1,128)S(1)}, u32[]{:S(2)}, u32[]{:S(2)}) %collective-permute-start.2) | collective-permute-done | bytes 97312 | tf_op jit(solution)/shard_map/ppermute | solution.py:42
  22.6 2.1 select_maximum_fusion.8
  26.1 1.9 collective-permute-start.5
  28.0 5.8 %collective-permute-start.4 = (f32[19,1,16,128]{3,2,1,0:T(8,128)S(1)}, f32[19,1,16,128]{3,2,1,0:T(8,128)S(1)}, u32[]{:S(2)}, u32[]{:S(2)}) collective-permute-start(f32[19,1,16,128]{3,2,1,0:T(8,128)S(1)} %get-tuple-element.60), channel_id=1, source_target_pairs={{16,0},{32,16},{48,32},{64,48},{80,64},{96,80},{112,96},{128,112},... | collective-permute-start | bytes 466952 | tf_op jit(solution)/shard_map/ppermute | solution.py:42
  34.8 1.8 collective-permute-done.4
  36.7 3.8 %collective-permute-start.7 = (f32[19,10,1,128]{3,2,1,0:T(1,128)S(1)}, f32[19,10,1,128]{3,2,1,0:T(1,128)S(1)}, u32[]{:S(2)}, u32[]{:S(2)}) collective-permute-start(f32[19,10,1,128]{3,2,1,0:T(1,128)S(1)} %get-tuple-element.53), channel_id=1, source_target_pairs={{0,1},{1,2},{2,3},{3,4},{4,5},{5,6},{6,7},{7,8},{8,9},{9,10},{10,1... | collective-permute-start | bytes 291848 | tf_op jit(solution)/shard_map/ppermute | solution.py:41
  42.7 5.3 %collective-permute-done.6 = f32[19,10,1,128]{3,2,1,0:T(1,128)S(1)} collective-permute-done((f32[19,10,1,128]{3,2,1,0:T(1,128)S(1)}, f32[19,10,1,128]{3,2,1,0:T(1,128)S(1)}, u32[]{:S(2)}, u32[]{:S(2)}) %collective-permute-start.6) | collective-permute-done | bytes 97312 | tf_op jit(solution)/shard_map/ppermute | solution.py:42
  48.0 4.3 %select_maximum_fusion.4 = f32[19,10,18,130]{3,2,1,0:T(8,128)S(1)} fusion(f32[19,10,1,128]{3,2,1,0:T(1,128)S(1)} %collective-permute-done.6, f32[19,10,1,128]{3,2,1,0:T(1,128)S(1)} %collective-permute-done.7, f32[19,1,16,128]{3,2,1,0:T(8,128)S(1)} %collective-permute-done.4, f32[19,8,16,128]{3,2,1,0:T(8,128)S(1)} %constant_dynamic-update-slice_fusion.3, ...), kind=kLoop, calls=%fused_computation.6 | loop fusion | flops 5335200 | bytes 3529440 | tf_op jit(solution)/shard_map/concatenate | solution.py:43
  53.6 1.9 collective-permute-start.9
  55.5 5.8 %collective-permute-start.8 = (f32[19,1,16,128]{3,2,1,0:T(8,128)S(1)}, f32[19,1,16,128]{3,2,1,0:T(8,128)S(1)}, u32[]{:S(2)}, u32[]{:S(2)}) collective-permute-start(f32[19,1,16,128]{3,2,1,0:T(8,128)S(1)} %get-tuple-element.58), channel_id=1, source_target_pairs={{16,0},{32,16},{48,32},{64,48},{80,64},{96,80},{112,96},{128,112},... | collective-permute-start | bytes 466952 | tf_op jit(solution)/shard_map/ppermute | solution.py:42
  64.1 5.1 %collective-permute-start.11 = (f32[19,10,1,128]{3,2,1,0:T(1,128)S(1)}, f32[19,10,1,128]{3,2,1,0:T(1,128)S(1)}, u32[]{:S(2)}, u32[]{:S(2)}) collective-permute-start(f32[19,10,1,128]{3,2,1,0:T(1,128)S(1)} %get-tuple-element.51), channel_id=1, source_target_pairs={{0,1},{1,2},{2,3},{3,4},{4,5},{5,6},{6,7},{7,8},{8,9},{9,10},{10,1... | collective-permute-start | bytes 291848 | tf_op jit(solution)/shard_map/ppermute | solution.py:41
  71.4 4.5 %collective-permute-done.10 = f32[19,10,1,128]{3,2,1,0:T(1,128)S(1)} collective-permute-done((f32[19,10,1,128]{3,2,1,0:T(1,128)S(1)}, f32[19,10,1,128]{3,2,1,0:T(1,128)S(1)}, u32[]{:S(2)}, u32[]{:S(2)}) %collective-permute-start.10) | collective-permute-done | bytes 97312 | tf_op jit(solution)/shard_map/ppermute | solution.py:42
  75.9 4.3 %select_maximum_fusion = f32[19,10,18,130]{3,2,1,0:T(8,128)S(1)} fusion(f32[19,10,1,128]{3,2,1,0:T(1,128)S(1)} %collective-permute-done.10, f32[19,10,1,128]{3,2,1,0:T(1,128)S(1)} %collective-permute-done.11, f32[19,1,16,128]{3,2,1,0:T(8,128)S(1)} %collective-permute-done.8, f32[19,8,16,128]{3,2,1,0:T(8,128)S(1)} %constant_dynamic-update-slice_fusion.22, ...), kind=kLoop, calls=%fused_computation.2 | loop fusion | flops 5335200 | bytes 3529440 | tf_op jit(solution)/shard_map/concatenate | solution.py:43
  80.9 1.9 collective-permute-start.13
  82.9 5.8 %collective-permute-start.12 = (f32[1,16,128]{2,1,0:T(8,128)S(1)}, f32[1,16,128]{2,1,0:T(8,128)S(1)}, u32[]{:S(2)}, u32[]{:S(2)}) collective-permute-start(f32[1,16,128]{2,1,0:T(8,128)S(1)} %get-tuple-element.94), channel_id=1, source_target_pairs={{16,0},{32,16},{48,32},{64,48},{80,64},{96,80},{112,96},{128,112},... | collective-permute-start | bytes 24584 | tf_op jit(solution)/shard_map/ppermute | solution.py:42
  90.0 3.9 %collective-permute-start.15 = (f32[10,1,128]{2,1,0:T(1,128)S(1)}, f32[10,1,128]{2,1,0:T(1,128)S(1)}, u32[]{:S(2)}, u32[]{:S(2)}) collective-permute-start(f32[10,1,128]{2,1,0:T(1,128)S(1)} %get-tuple-element.77), channel_id=1, source_target_pairs={{0,1},{1,2},{2,3},{3,4},{4,5},{5,6},{6,7},{7,8},{8,9},{9,10},{10,1... | collective-permute-start | bytes 15368 | tf_op jit(solution)/shard_map/ppermute | solution.py:41
  95.3 4.2 %collective-permute-done.14 = f32[10,1,128]{2,1,0:T(1,128)S(1)} collective-permute-done((f32[10,1,128]{2,1,0:T(1,128)S(1)}, f32[10,1,128]{2,1,0:T(1,128)S(1)}, u32[]{:S(2)}, u32[]{:S(2)}) %collective-permute-start.14) | collective-permute-done | bytes 5152 | tf_op jit(solution)/shard_map/ppermute | solution.py:42
  99.7 1.9 collective-permute-start.17
  101.7 5.9 %collective-permute-start.16 = (f32[1,16,128]{2,1,0:T(8,128)S(1)}, f32[1,16,128]{2,1,0:T(8,128)S(1)}, u32[]{:S(2)}, u32[]{:S(2)}) collective-permute-start(f32[1,16,128]{2,1,0:T(8,128)S(1)} %get-tuple-element.92), channel_id=1, source_target_pairs={{16,0},{32,16},{48,32},{64,48},{80,64},{96,80},{112,96},{128,112},... | collective-permute-start | bytes 24584 | tf_op jit(solution)/shard_map/ppermute | solution.py:42
  108.8 4.7 %collective-permute-start.19 = (f32[10,1,128]{2,1,0:T(1,128)S(1)}, f32[10,1,128]{2,1,0:T(1,128)S(1)}, u32[]{:S(2)}, u32[]{:S(2)}) collective-permute-start(f32[10,1,128]{2,1,0:T(1,128)S(1)} %get-tuple-element.75), channel_id=1, source_target_pairs={{0,1},{1,2},{2,3},{3,4},{4,5},{5,6},{6,7},{7,8},{8,9},{9,10},{10,1... | collective-permute-start | bytes 15368 | tf_op jit(solution)/shard_map/ppermute | solution.py:41
  114.9 4.2 %collective-permute-done.18 = f32[10,1,128]{2,1,0:T(1,128)S(1)} collective-permute-done((f32[10,1,128]{2,1,0:T(1,128)S(1)}, f32[10,1,128]{2,1,0:T(1,128)S(1)}, u32[]{:S(2)}, u32[]{:S(2)}) %collective-permute-start.18) | collective-permute-done | bytes 5152 | tf_op jit(solution)/shard_map/ppermute | solution.py:42
  119.3 1.9 collective-permute-start.21
  121.3 5.8 %collective-permute-start.20 = (f32[1,16,128]{2,1,0:T(8,128)S(1)}, f32[1,16,128]{2,1,0:T(8,128)S(1)}, u32[]{:S(2)}, u32[]{:S(2)}) collective-permute-start(f32[1,16,128]{2,1,0:T(8,128)S(1)} %get-tuple-element.90), channel_id=1, source_target_pairs={{16,0},{32,16},{48,32},{64,48},{80,64},{96,80},{112,96},{128,112},... | collective-permute-start | bytes 24584 | tf_op jit(solution)/shard_map/ppermute | solution.py:42
  128.4 5.1 %collective-permute-start.23 = (f32[10,1,128]{2,1,0:T(1,128)S(1)}, f32[10,1,128]{2,1,0:T(1,128)S(1)}, u32[]{:S(2)}, u32[]{:S(2)}) collective-permute-start(f32[10,1,128]{2,1,0:T(1,128)S(1)} %get-tuple-element.73), channel_id=1, source_target_pairs={{0,1},{1,2},{2,3},{3,4},{4,5},{5,6},{6,7},{7,8},{8,9},{9,10},{10,1... | collective-permute-start | bytes 15368 | tf_op jit(solution)/shard_map/ppermute | solution.py:41
  134.9 4.2 %collective-permute-done.22 = f32[10,1,128]{2,1,0:T(1,128)S(1)} collective-permute-done((f32[10,1,128]{2,1,0:T(1,128)S(1)}, f32[10,1,128]{2,1,0:T(1,128)S(1)}, u32[]{:S(2)}, u32[]{:S(2)}) %collective-permute-start.22) | collective-permute-done | bytes 5152 | tf_op jit(solution)/shard_map/ppermute | solution.py:42
  139.3 1.9 collective-permute-start.25
  141.3 5.8 %collective-permute-start.24 = (f32[1,16,128]{2,1,0:T(8,128)S(1)}, f32[1,16,128]{2,1,0:T(8,128)S(1)}, u32[]{:S(2)}, u32[]{:S(2)}) collective-permute-start(f32[1,16,128]{2,1,0:T(8,128)S(1)} %get-tuple-element.88), channel_id=1, source_target_pairs={{16,0},{32,16},{48,32},{64,48},{80,64},{96,80},{112,96},{128,112},... | collective-permute-start | bytes 24584 | tf_op jit(solution)/shard_map/ppermute | solution.py:42
  148.4 3.9 %collective-permute-start.27 = (f32[10,1,128]{2,1,0:T(1,128)S(1)}, f32[10,1,128]{2,1,0:T(1,128)S(1)}, u32[]{:S(2)}, u32[]{:S(2)}) collective-permute-start(f32[10,1,128]{2,1,0:T(1,128)S(1)} %get-tuple-element.71), channel_id=1, source_target_pairs={{0,1},{1,2},{2,3},{3,4},{4,5},{5,6},{6,7},{7,8},{8,9},{9,10},{10,1... | collective-permute-start | bytes 15368 | tf_op jit(solution)/shard_map/ppermute | solution.py:41
  153.6 4.2 %collective-permute-done.26 = f32[10,1,128]{2,1,0:T(1,128)S(1)} collective-permute-done((f32[10,1,128]{2,1,0:T(1,128)S(1)}, f32[10,1,128]{2,1,0:T(1,128)S(1)}, u32[]{:S(2)}, u32[]{:S(2)}) %collective-permute-start.26) | collective-permute-done | bytes 5152 | tf_op jit(solution)/shard_map/ppermute | solution.py:42
  158.1 1.9 collective-permute-start.29
  160.0 5.8 %collective-permute-start.28 = (f32[1,16,128]{2,1,0:T(8,128)S(1)}, f32[1,16,128]{2,1,0:T(8,128)S(1)}, u32[]{:S(2)}, u32[]{:S(2)}) collective-permute-start(f32[1,16,128]{2,1,0:T(8,128)S(1)} %get-tuple-element.86), channel_id=1, source_target_pairs={{16,0},{32,16},{48,32},{64,48},{80,64},{96,80},{112,96},{128,112},... | collective-permute-start | bytes 24584 | tf_op jit(solution)/shard_map/ppermute | solution.py:42
  167.1 3.9 %collective-permute-start.31 = (f32[10,1,128]{2,1,0:T(1,128)S(1)}, f32[10,1,128]{2,1,0:T(1,128)S(1)}, u32[]{:S(2)}, u32[]{:S(2)}) collective-permute-start(f32[10,1,128]{2,1,0:T(1,128)S(1)} %get-tuple-element.69), channel_id=1, source_target_pairs={{0,1},{1,2},{2,3},{3,4},{4,5},{5,6},{6,7},{7,8},{8,9},{9,10},{10,1... | collective-permute-start | bytes 15368 | tf_op jit(solution)/shard_map/ppermute | solution.py:41
  172.4 4.2 %collective-permute-done.30 = f32[10,1,128]{2,1,0:T(1,128)S(1)} collective-permute-done((f32[10,1,128]{2,1,0:T(1,128)S(1)}, f32[10,1,128]{2,1,0:T(1,128)S(1)}, u32[]{:S(2)}, u32[]{:S(2)}) %collective-permute-start.30) | collective-permute-done | bytes 5152 | tf_op jit(solution)/shard_map/ppermute | solution.py:42
  176.9 1.9 collective-permute-start.33
  178.8 5.8 %collective-permute-start.32 = (f32[1,16,128]{2,1,0:T(8,128)S(1)}, f32[1,16,128]{2,1,0:T(8,128)S(1)}, u32[]{:S(2)}, u32[]{:S(2)}) collective-permute-start(f32[1,16,128]{2,1,0:T(8,128)S(1)} %get-tuple-element.84), channel_id=1, source_target_pairs={{16,0},{32,16},{48,32},{64,48},{80,64},{96,80},{112,96},{128,112},... | collective-permute-start | bytes 24584 | tf_op jit(solution)/shard_map/ppermute | solution.py:42
  185.9 3.1 %collective-permute-start.35 = (f32[10,1,128]{2,1,0:T(1,128)S(1)}, f32[10,1,128]{2,1,0:T(1,128)S(1)}, u32[]{:S(2)}, u32[]{:S(2)}) collective-permute-start(f32[10,1,128]{2,1,0:T(1,128)S(1)} %get-tuple-element.67), channel_id=1, source_target_pairs={{0,1},{1,2},{2,3},{3,4},{4,5},{5,6},{6,7},{7,8},{8,9},{9,10},{10,1... | collective-permute-start | bytes 15368 | tf_op jit(solution)/shard_map/ppermute | solution.py:41
  190.5 4.1 %collective-permute-done.34 = f32[10,1,128]{2,1,0:T(1,128)S(1)} collective-permute-done((f32[10,1,128]{2,1,0:T(1,128)S(1)}, f32[10,1,128]{2,1,0:T(1,128)S(1)}, u32[]{:S(2)}, u32[]{:S(2)}) %collective-permute-start.34) | collective-permute-done | bytes 5152 | tf_op jit(solution)/shard_map/ppermute | solution.py:42
  194.9 1.9 collective-permute-start.37
  196.8 5.8 %collective-permute-start.36 = (f32[1,16,128]{2,1,0:T(8,128)S(1)}, f32[1,16,128]{2,1,0:T(8,128)S(1)}, u32[]{:S(2)}, u32[]{:S(2)}) collective-permute-start(f32[1,16,128]{2,1,0:T(8,128)S(1)} %get-tuple-element.82), channel_id=1, source_target_pairs={{16,0},{32,16},{48,32},{64,48},{80,64},{96,80},{112,96},{128,112},... | collective-permute-start | bytes 24584 | tf_op jit(solution)/shard_map/ppermute | solution.py:42
  203.9 3.1 %collective-permute-start.39 = (f32[10,1,128]{2,1,0:T(1,128)S(1)}, f32[10,1,128]{2,1,0:T(1,128)S(1)}, u32[]{:S(2)}, u32[]{:S(2)}) collective-permute-start(f32[10,1,128]{2,1,0:T(1,128)S(1)} %get-tuple-element.65), channel_id=1, source_target_pairs={{0,1},{1,2},{2,3},{3,4},{4,5},{5,6},{6,7},{7,8},{8,9},{9,10},{10,1... | collective-permute-start | bytes 15368 | tf_op jit(solution)/shard_map/ppermute | solution.py:41
  208.4 4.2 %collective-permute-done.38 = f32[10,1,128]{2,1,0:T(1,128)S(1)} collective-permute-done((f32[10,1,128]{2,1,0:T(1,128)S(1)}, f32[10,1,128]{2,1,0:T(1,128)S(1)}, u32[]{:S(2)}, u32[]{:S(2)}) %collective-permute-start.38) | collective-permute-done | bytes 5152 | tf_op jit(solution)/shard_map/ppermute | solution.py:42
  212.9 1.9 collective-permute-start.41
  214.8 5.8 %collective-permute-start.40 = (f32[1,16,128]{2,1,0:T(8,128)S(1)}, f32[1,16,128]{2,1,0:T(8,128)S(1)}, u32[]{:S(2)}, u32[]{:S(2)}) collective-permute-start(f32[1,16,128]{2,1,0:T(8,128)S(1)} %get-tuple-element.80), channel_id=1, source_target_pairs={{16,0},{32,16},{48,32},{64,48},{80,64},{96,80},{112,96},{128,112},... | collective-permute-start | bytes 24584 | tf_op jit(solution)/shard_map/ppermute | solution.py:42
  221.9 3.1 %collective-permute-start.43 = (f32[10,1,128]{2,1,0:T(1,128)S(1)}, f32[10,1,128]{2,1,0:T(1,128)S(1)}, u32[]{:S(2)}, u32[]{:S(2)}) collective-permute-start(f32[10,1,128]{2,1,0:T(1,128)S(1)} %get-tuple-element.63), channel_id=1, source_target_pairs={{0,1},{1,2},{2,3},{3,4},{4,5},{5,6},{6,7},{7,8},{8,9},{9,10},{10,1... | collective-permute-start | bytes 15368 | tf_op jit(solution)/shard_map/ppermute | solution.py:41
  226.5 4.1 %collective-permute-done.42 = f32[10,1,128]{2,1,0:T(1,128)S(1)} collective-permute-done((f32[10,1,128]{2,1,0:T(1,128)S(1)}, f32[10,1,128]{2,1,0:T(1,128)S(1)}, u32[]{:S(2)}, u32[]{:S(2)}) %collective-permute-start.42) | collective-permute-done | bytes 5152 | tf_op jit(solution)/shard_map/ppermute | solution.py:42
  (158 shorter events, 41.5 us)
Async XLA Ops:
  1.7 8.7 %collective-permute-start.1 = (f32[19,1,16,128]{3,2,1,0:T(8,128)S(1)}, f32[19,1,16,128]{3,2,1,0:T(8,128)S(1)}, u32[]{:S(2)}, u32[]{:S(2)}) collective-permute-start(f32[19,1,16,128]{3,2,1,0:T(8,128)S(1)} %get-tuple-element.62), channel_id=1, source_target_pairs={{0,16},{16,32},{32,48},{48,64},{64,80},{80,96},{96,112},{112,128},... | collective-permute-start | bytes 466952 | tf_op jit(solution)/shard_map/ppermute | solution.py:41
  3.6 8.5 %collective-permute-start = (f32[19,1,16,128]{3,2,1,0:T(8,128)S(1)}, f32[19,1,16,128]{3,2,1,0:T(8,128)S(1)}, u32[]{:S(2)}, u32[]{:S(2)}) collective-permute-start(f32[19,1,16,128]{3,2,1,0:T(8,128)S(1)} %get-tuple-element.61), channel_id=1, source_target_pairs={{16,0},{32,16},{48,32},{64,48},{80,64},{96,80},{112,96},{128,112},... | collective-permute-start | bytes 466952 | tf_op jit(solution)/shard_map/ppermute | solution.py:42
  12.2 6.0 %collective-permute-start.3 = (f32[19,10,1,128]{3,2,1,0:T(1,128)S(1)}, f32[19,10,1,128]{3,2,1,0:T(1,128)S(1)}, u32[]{:S(2)}, u32[]{:S(2)}) collective-permute-start(f32[19,10,1,128]{3,2,1,0:T(1,128)S(1)} %get-tuple-element.55), channel_id=1, source_target_pairs={{0,1},{1,2},{2,3},{3,4},{4,5},{5,6},{6,7},{7,8},{8,9},{9,10},{10,1... | collective-permute-start | bytes 291848 | tf_op jit(solution)/shard_map/ppermute | solution.py:41
  16.1 6.5 %collective-permute-start.2 = (f32[19,10,1,128]{3,2,1,0:T(1,128)S(1)}, f32[19,10,1,128]{3,2,1,0:T(1,128)S(1)}, u32[]{:S(2)}, u32[]{:S(2)}) collective-permute-start(f32[19,10,1,128]{3,2,1,0:T(1,128)S(1)} %get-tuple-element.56), channel_id=1, source_target_pairs={{1,0},{2,1},{3,2},{4,3},{5,4},{6,5},{7,6},{8,7},{9,8},{10,9},{11,1... | collective-permute-start | bytes 291848 | tf_op jit(solution)/shard_map/ppermute | solution.py:42
  17.4 7.3 %copy-start = (s32[8,16,128]{2,1,0:T(8,128)S(1)}, s32[8,16,128]{2,1,0:T(8,128)}, u32[]{:S(2)}) copy-start(s32[8,16,128]{2,1,0:T(8,128)} %param.10) | copy-start | bytes 196612
  17.4 7.3 %copy-start.1 = (f32[8,16,128]{2,1,0:T(8,128)S(1)}, f32[8,16,128]{2,1,0:T(8,128)}, u32[]{:S(2)}) copy-start(f32[8,16,128]{2,1,0:T(8,128)} %param.9) | copy-start | bytes 196612
  26.1 8.7 %collective-permute-start.5 = (f32[19,1,16,128]{3,2,1,0:T(8,128)S(1)}, f32[19,1,16,128]{3,2,1,0:T(8,128)S(1)}, u32[]{:S(2)}, u32[]{:S(2)}) collective-permute-start(f32[19,1,16,128]{3,2,1,0:T(8,128)S(1)} %get-tuple-element.59), channel_id=1, source_target_pairs={{0,16},{16,32},{32,48},{48,64},{64,80},{80,96},{96,112},{112,128},... | collective-permute-start | bytes 466952 | tf_op jit(solution)/shard_map/ppermute | solution.py:41
  28.0 8.5 %collective-permute-start.4 = (f32[19,1,16,128]{3,2,1,0:T(8,128)S(1)}, f32[19,1,16,128]{3,2,1,0:T(8,128)S(1)}, u32[]{:S(2)}, u32[]{:S(2)}) collective-permute-start(f32[19,1,16,128]{3,2,1,0:T(8,128)S(1)} %get-tuple-element.60), channel_id=1, source_target_pairs={{16,0},{32,16},{48,32},{64,48},{80,64},{96,80},{112,96},{128,112},... | collective-permute-start | bytes 466952 | tf_op jit(solution)/shard_map/ppermute | solution.py:42
  36.7 6.0 %collective-permute-start.7 = (f32[19,10,1,128]{3,2,1,0:T(1,128)S(1)}, f32[19,10,1,128]{3,2,1,0:T(1,128)S(1)}, u32[]{:S(2)}, u32[]{:S(2)}) collective-permute-start(f32[19,10,1,128]{3,2,1,0:T(1,128)S(1)} %get-tuple-element.53), channel_id=1, source_target_pairs={{0,1},{1,2},{2,3},{3,4},{4,5},{5,6},{6,7},{7,8},{8,9},{9,10},{10,1... | collective-permute-start | bytes 291848 | tf_op jit(solution)/shard_map/ppermute | solution.py:41
  40.5 7.5 %collective-permute-start.6 = (f32[19,10,1,128]{3,2,1,0:T(1,128)S(1)}, f32[19,10,1,128]{3,2,1,0:T(1,128)S(1)}, u32[]{:S(2)}, u32[]{:S(2)}) collective-permute-start(f32[19,10,1,128]{3,2,1,0:T(1,128)S(1)} %get-tuple-element.54), channel_id=1, source_target_pairs={{1,0},{2,1},{3,2},{4,3},{5,4},{6,5},{7,6},{8,7},{9,8},{10,9},{11,1... | collective-permute-start | bytes 291848 | tf_op jit(solution)/shard_map/ppermute | solution.py:42
  53.6 8.7 %collective-permute-start.9 = (f32[19,1,16,128]{3,2,1,0:T(8,128)S(1)}, f32[19,1,16,128]{3,2,1,0:T(8,128)S(1)}, u32[]{:S(2)}, u32[]{:S(2)}) collective-permute-start(f32[19,1,16,128]{3,2,1,0:T(8,128)S(1)} %get-tuple-element.57), channel_id=1, source_target_pairs={{0,16},{16,32},{32,48},{48,64},{64,80},{80,96},{96,112},{112,128},... | collective-permute-start | bytes 466952 | tf_op jit(solution)/shard_map/ppermute | solution.py:41
  55.5 8.5 %collective-permute-start.8 = (f32[19,1,16,128]{3,2,1,0:T(8,128)S(1)}, f32[19,1,16,128]{3,2,1,0:T(8,128)S(1)}, u32[]{:S(2)}, u32[]{:S(2)}) collective-permute-start(f32[19,1,16,128]{3,2,1,0:T(8,128)S(1)} %get-tuple-element.58), channel_id=1, source_target_pairs={{16,0},{32,16},{48,32},{64,48},{80,64},{96,80},{112,96},{128,112},... | collective-permute-start | bytes 466952 | tf_op jit(solution)/shard_map/ppermute | solution.py:42
  64.1 7.3 %collective-permute-start.11 = (f32[19,10,1,128]{3,2,1,0:T(1,128)S(1)}, f32[19,10,1,128]{3,2,1,0:T(1,128)S(1)}, u32[]{:S(2)}, u32[]{:S(2)}) collective-permute-start(f32[19,10,1,128]{3,2,1,0:T(1,128)S(1)} %get-tuple-element.51), channel_id=1, source_target_pairs={{0,1},{1,2},{2,3},{3,4},{4,5},{5,6},{6,7},{7,8},{8,9},{9,10},{10,1... | collective-permute-start | bytes 291848 | tf_op jit(solution)/shard_map/ppermute | solution.py:41
  69.3 10.9 %copy-start.5 = (f32[8,16,128]{2,1,0:T(8,128)S(1)}, f32[8,16,128]{2,1,0:T(8,128)}, u32[]{:S(2)}) copy-start(f32[8,16,128]{2,1,0:T(8,128)} %param.8) | copy-start | bytes 196612
  69.3 6.6 %collective-permute-start.10 = (f32[19,10,1,128]{3,2,1,0:T(1,128)S(1)}, f32[19,10,1,128]{3,2,1,0:T(1,128)S(1)}, u32[]{:S(2)}, u32[]{:S(2)}) collective-permute-start(f32[19,10,1,128]{3,2,1,0:T(1,128)S(1)} %get-tuple-element.52), channel_id=1, source_target_pairs={{1,0},{2,1},{3,2},{4,3},{5,4},{6,5},{7,6},{8,7},{9,8},{10,9},{11,1... | collective-permute-start | bytes 291848 | tf_op jit(solution)/shard_map/ppermute | solution.py:42
  80.9 18.7 %copy-start.3 = (s32[8,16,128]{2,1,0:T(8,128)S(1)}, s32[8,16,128]{2,1,0:T(8,128)}, u32[]{:S(2)}) copy-start(s32[8,16,128]{2,1,0:T(8,128)} %param.11) | copy-start | bytes 196612
  80.9 7.8 %collective-permute-start.13 = (f32[1,16,128]{2,1,0:T(8,128)S(1)}, f32[1,16,128]{2,1,0:T(8,128)S(1)}, u32[]{:S(2)}, u32[]{:S(2)}) collective-permute-start(f32[1,16,128]{2,1,0:T(8,128)S(1)} %get-tuple-element.93), channel_id=1, source_target_pairs={{0,16},{16,32},{32,48},{48,64},{64,80},{80,96},{96,112},{112,128},... | collective-permute-start | bytes 24584 | tf_op jit(solution)/shard_map/ppermute | solution.py:41
  82.9 7.1 %collective-permute-start.12 = (f32[1,16,128]{2,1,0:T(8,128)S(1)}, f32[1,16,128]{2,1,0:T(8,128)S(1)}, u32[]{:S(2)}, u32[]{:S(2)}) collective-permute-start(f32[1,16,128]{2,1,0:T(8,128)S(1)} %get-tuple-element.94), channel_id=1, source_target_pairs={{16,0},{32,16},{48,32},{64,48},{80,64},{96,80},{112,96},{128,112},... | collective-permute-start | bytes 24584 | tf_op jit(solution)/shard_map/ppermute | solution.py:42
  90.0 5.3 %collective-permute-start.15 = (f32[10,1,128]{2,1,0:T(1,128)S(1)}, f32[10,1,128]{2,1,0:T(1,128)S(1)}, u32[]{:S(2)}, u32[]{:S(2)}) collective-permute-start(f32[10,1,128]{2,1,0:T(1,128)S(1)} %get-tuple-element.77), channel_id=1, source_target_pairs={{0,1},{1,2},{2,3},{3,4},{4,5},{5,6},{6,7},{7,8},{8,9},{9,10},{10,1... | collective-permute-start | bytes 15368 | tf_op jit(solution)/shard_map/ppermute | solution.py:41
  93.9 5.5 %collective-permute-start.14 = (f32[10,1,128]{2,1,0:T(1,128)S(1)}, f32[10,1,128]{2,1,0:T(1,128)S(1)}, u32[]{:S(2)}, u32[]{:S(2)}) collective-permute-start(f32[10,1,128]{2,1,0:T(1,128)S(1)} %get-tuple-element.78), channel_id=1, source_target_pairs={{1,0},{2,1},{3,2},{4,3},{5,4},{6,5},{7,6},{8,7},{9,8},{10,9},{11,1... | collective-permute-start | bytes 15368 | tf_op jit(solution)/shard_map/ppermute | solution.py:42
  99.7 8.0 %collective-permute-start.17 = (f32[1,16,128]{2,1,0:T(8,128)S(1)}, f32[1,16,128]{2,1,0:T(8,128)S(1)}, u32[]{:S(2)}, u32[]{:S(2)}) collective-permute-start(f32[1,16,128]{2,1,0:T(8,128)S(1)} %get-tuple-element.91), channel_id=1, source_target_pairs={{0,16},{16,32},{32,48},{48,64},{64,80},{80,96},{96,112},{112,128},... | collective-permute-start | bytes 24584 | tf_op jit(solution)/shard_map/ppermute | solution.py:41
  101.7 7.1 %collective-permute-start.16 = (f32[1,16,128]{2,1,0:T(8,128)S(1)}, f32[1,16,128]{2,1,0:T(8,128)S(1)}, u32[]{:S(2)}, u32[]{:S(2)}) collective-permute-start(f32[1,16,128]{2,1,0:T(8,128)S(1)} %get-tuple-element.92), channel_id=1, source_target_pairs={{16,0},{32,16},{48,32},{64,48},{80,64},{96,80},{112,96},{128,112},... | collective-permute-start | bytes 24584 | tf_op jit(solution)/shard_map/ppermute | solution.py:42
  108.8 6.1 %collective-permute-start.19 = (f32[10,1,128]{2,1,0:T(1,128)S(1)}, f32[10,1,128]{2,1,0:T(1,128)S(1)}, u32[]{:S(2)}, u32[]{:S(2)}) collective-permute-start(f32[10,1,128]{2,1,0:T(1,128)S(1)} %get-tuple-element.75), channel_id=1, source_target_pairs={{0,1},{1,2},{2,3},{3,4},{4,5},{5,6},{6,7},{7,8},{8,9},{9,10},{10,1... | collective-permute-start | bytes 15368 | tf_op jit(solution)/shard_map/ppermute | solution.py:41
  113.5 5.5 %collective-permute-start.18 = (f32[10,1,128]{2,1,0:T(1,128)S(1)}, f32[10,1,128]{2,1,0:T(1,128)S(1)}, u32[]{:S(2)}, u32[]{:S(2)}) collective-permute-start(f32[10,1,128]{2,1,0:T(1,128)S(1)} %get-tuple-element.76), channel_id=1, source_target_pairs={{1,0},{2,1},{3,2},{4,3},{5,4},{6,5},{7,6},{8,7},{9,8},{10,9},{11,1... | collective-permute-start | bytes 15368 | tf_op jit(solution)/shard_map/ppermute | solution.py:42
  119.3 7.7 %collective-permute-start.21 = (f32[1,16,128]{2,1,0:T(8,128)S(1)}, f32[1,16,128]{2,1,0:T(8,128)S(1)}, u32[]{:S(2)}, u32[]{:S(2)}) collective-permute-start(f32[1,16,128]{2,1,0:T(8,128)S(1)} %get-tuple-element.89), channel_id=1, source_target_pairs={{0,16},{16,32},{32,48},{48,64},{64,80},{80,96},{96,112},{112,128},... | collective-permute-start | bytes 24584 | tf_op jit(solution)/shard_map/ppermute | solution.py:41
  121.3 7.1 %collective-permute-start.20 = (f32[1,16,128]{2,1,0:T(8,128)S(1)}, f32[1,16,128]{2,1,0:T(8,128)S(1)}, u32[]{:S(2)}, u32[]{:S(2)}) collective-permute-start(f32[1,16,128]{2,1,0:T(8,128)S(1)} %get-tuple-element.90), channel_id=1, source_target_pairs={{16,0},{32,16},{48,32},{64,48},{80,64},{96,80},{112,96},{128,112},... | collective-permute-start | bytes 24584 | tf_op jit(solution)/shard_map/ppermute | solution.py:42
  128.4 6.5 %collective-permute-start.23 = (f32[10,1,128]{2,1,0:T(1,128)S(1)}, f32[10,1,128]{2,1,0:T(1,128)S(1)}, u32[]{:S(2)}, u32[]{:S(2)}) collective-permute-start(f32[10,1,128]{2,1,0:T(1,128)S(1)} %get-tuple-element.73), channel_id=1, source_target_pairs={{0,1},{1,2},{2,3},{3,4},{4,5},{5,6},{6,7},{7,8},{8,9},{9,10},{10,1... | collective-permute-start | bytes 15368 | tf_op jit(solution)/shard_map/ppermute | solution.py:41
  133.5 5.5 %collective-permute-start.22 = (f32[10,1,128]{2,1,0:T(1,128)S(1)}, f32[10,1,128]{2,1,0:T(1,128)S(1)}, u32[]{:S(2)}, u32[]{:S(2)}) collective-permute-start(f32[10,1,128]{2,1,0:T(1,128)S(1)} %get-tuple-element.74), channel_id=1, source_target_pairs={{1,0},{2,1},{3,2},{4,3},{5,4},{6,5},{7,6},{8,7},{9,8},{10,9},{11,1... | collective-permute-start | bytes 15368 | tf_op jit(solution)/shard_map/ppermute | solution.py:42
  139.3 7.7 %collective-permute-start.25 = (f32[1,16,128]{2,1,0:T(8,128)S(1)}, f32[1,16,128]{2,1,0:T(8,128)S(1)}, u32[]{:S(2)}, u32[]{:S(2)}) collective-permute-start(f32[1,16,128]{2,1,0:T(8,128)S(1)} %get-tuple-element.87), channel_id=1, source_target_pairs={{0,16},{16,32},{32,48},{48,64},{64,80},{80,96},{96,112},{112,128},... | collective-permute-start | bytes 24584 | tf_op jit(solution)/shard_map/ppermute | solution.py:41
  141.3 7.1 %collective-permute-start.24 = (f32[1,16,128]{2,1,0:T(8,128)S(1)}, f32[1,16,128]{2,1,0:T(8,128)S(1)}, u32[]{:S(2)}, u32[]{:S(2)}) collective-permute-start(f32[1,16,128]{2,1,0:T(8,128)S(1)} %get-tuple-element.88), channel_id=1, source_target_pairs={{16,0},{32,16},{48,32},{64,48},{80,64},{96,80},{112,96},{128,112},... | collective-permute-start | bytes 24584 | tf_op jit(solution)/shard_map/ppermute | solution.py:42
  148.4 5.3 %collective-permute-start.27 = (f32[10,1,128]{2,1,0:T(1,128)S(1)}, f32[10,1,128]{2,1,0:T(1,128)S(1)}, u32[]{:S(2)}, u32[]{:S(2)}) collective-permute-start(f32[10,1,128]{2,1,0:T(1,128)S(1)} %get-tuple-element.71), channel_id=1, source_target_pairs={{0,1},{1,2},{2,3},{3,4},{4,5},{5,6},{6,7},{7,8},{8,9},{9,10},{10,1... | collective-permute-start | bytes 15368 | tf_op jit(solution)/shard_map/ppermute | solution.py:41
  152.3 5.5 %collective-permute-start.26 = (f32[10,1,128]{2,1,0:T(1,128)S(1)}, f32[10,1,128]{2,1,0:T(1,128)S(1)}, u32[]{:S(2)}, u32[]{:S(2)}) collective-permute-start(f32[10,1,128]{2,1,0:T(1,128)S(1)} %get-tuple-element.72), channel_id=1, source_target_pairs={{1,0},{2,1},{3,2},{4,3},{5,4},{6,5},{7,6},{8,7},{9,8},{10,9},{11,1... | collective-permute-start | bytes 15368 | tf_op jit(solution)/shard_map/ppermute | solution.py:42
  158.1 7.8 %collective-permute-start.29 = (f32[1,16,128]{2,1,0:T(8,128)S(1)}, f32[1,16,128]{2,1,0:T(8,128)S(1)}, u32[]{:S(2)}, u32[]{:S(2)}) collective-permute-start(f32[1,16,128]{2,1,0:T(8,128)S(1)} %get-tuple-element.85), channel_id=1, source_target_pairs={{0,16},{16,32},{32,48},{48,64},{64,80},{80,96},{96,112},{112,128},... | collective-permute-start | bytes 24584 | tf_op jit(solution)/shard_map/ppermute | solution.py:41
  160.0 7.1 %collective-permute-start.28 = (f32[1,16,128]{2,1,0:T(8,128)S(1)}, f32[1,16,128]{2,1,0:T(8,128)S(1)}, u32[]{:S(2)}, u32[]{:S(2)}) collective-permute-start(f32[1,16,128]{2,1,0:T(8,128)S(1)} %get-tuple-element.86), channel_id=1, source_target_pairs={{16,0},{32,16},{48,32},{64,48},{80,64},{96,80},{112,96},{128,112},... | collective-permute-start | bytes 24584 | tf_op jit(solution)/shard_map/ppermute | solution.py:42
  167.1 5.3 %collective-permute-start.31 = (f32[10,1,128]{2,1,0:T(1,128)S(1)}, f32[10,1,128]{2,1,0:T(1,128)S(1)}, u32[]{:S(2)}, u32[]{:S(2)}) collective-permute-start(f32[10,1,128]{2,1,0:T(1,128)S(1)} %get-tuple-element.69), channel_id=1, source_target_pairs={{0,1},{1,2},{2,3},{3,4},{4,5},{5,6},{6,7},{7,8},{8,9},{9,10},{10,1... | collective-permute-start | bytes 15368 | tf_op jit(solution)/shard_map/ppermute | solution.py:41
  171.1 5.5 %collective-permute-start.30 = (f32[10,1,128]{2,1,0:T(1,128)S(1)}, f32[10,1,128]{2,1,0:T(1,128)S(1)}, u32[]{:S(2)}, u32[]{:S(2)}) collective-permute-start(f32[10,1,128]{2,1,0:T(1,128)S(1)} %get-tuple-element.70), channel_id=1, source_target_pairs={{1,0},{2,1},{3,2},{4,3},{5,4},{6,5},{7,6},{8,7},{9,8},{10,9},{11,1... | collective-permute-start | bytes 15368 | tf_op jit(solution)/shard_map/ppermute | solution.py:42
  176.9 7.7 %collective-permute-start.33 = (f32[1,16,128]{2,1,0:T(8,128)S(1)}, f32[1,16,128]{2,1,0:T(8,128)S(1)}, u32[]{:S(2)}, u32[]{:S(2)}) collective-permute-start(f32[1,16,128]{2,1,0:T(8,128)S(1)} %get-tuple-element.83), channel_id=1, source_target_pairs={{0,16},{16,32},{32,48},{48,64},{64,80},{80,96},{96,112},{112,128},... | collective-permute-start | bytes 24584 | tf_op jit(solution)/shard_map/ppermute | solution.py:41
  178.8 7.1 %collective-permute-start.32 = (f32[1,16,128]{2,1,0:T(8,128)S(1)}, f32[1,16,128]{2,1,0:T(8,128)S(1)}, u32[]{:S(2)}, u32[]{:S(2)}) collective-permute-start(f32[1,16,128]{2,1,0:T(8,128)S(1)} %get-tuple-element.84), channel_id=1, source_target_pairs={{16,0},{32,16},{48,32},{64,48},{80,64},{96,80},{112,96},{128,112},... | collective-permute-start | bytes 24584 | tf_op jit(solution)/shard_map/ppermute | solution.py:42
  185.9 4.5 %collective-permute-start.35 = (f32[10,1,128]{2,1,0:T(1,128)S(1)}, f32[10,1,128]{2,1,0:T(1,128)S(1)}, u32[]{:S(2)}, u32[]{:S(2)}) collective-permute-start(f32[10,1,128]{2,1,0:T(1,128)S(1)} %get-tuple-element.67), channel_id=1, source_target_pairs={{0,1},{1,2},{2,3},{3,4},{4,5},{5,6},{6,7},{7,8},{8,9},{9,10},{10,1... | collective-permute-start | bytes 15368 | tf_op jit(solution)/shard_map/ppermute | solution.py:41
  189.1 5.5 %collective-permute-start.34 = (f32[10,1,128]{2,1,0:T(1,128)S(1)}, f32[10,1,128]{2,1,0:T(1,128)S(1)}, u32[]{:S(2)}, u32[]{:S(2)}) collective-permute-start(f32[10,1,128]{2,1,0:T(1,128)S(1)} %get-tuple-element.68), channel_id=1, source_target_pairs={{1,0},{2,1},{3,2},{4,3},{5,4},{6,5},{7,6},{8,7},{9,8},{10,9},{11,1... | collective-permute-start | bytes 15368 | tf_op jit(solution)/shard_map/ppermute | solution.py:42
  194.9 7.8 %collective-permute-start.37 = (f32[1,16,128]{2,1,0:T(8,128)S(1)}, f32[1,16,128]{2,1,0:T(8,128)S(1)}, u32[]{:S(2)}, u32[]{:S(2)}) collective-permute-start(f32[1,16,128]{2,1,0:T(8,128)S(1)} %get-tuple-element.81), channel_id=1, source_target_pairs={{0,16},{16,32},{32,48},{48,64},{64,80},{80,96},{96,112},{112,128},... | collective-permute-start | bytes 24584 | tf_op jit(solution)/shard_map/ppermute | solution.py:41
  196.8 7.1 %collective-permute-start.36 = (f32[1,16,128]{2,1,0:T(8,128)S(1)}, f32[1,16,128]{2,1,0:T(8,128)S(1)}, u32[]{:S(2)}, u32[]{:S(2)}) collective-permute-start(f32[1,16,128]{2,1,0:T(8,128)S(1)} %get-tuple-element.82), channel_id=1, source_target_pairs={{16,0},{32,16},{48,32},{64,48},{80,64},{96,80},{112,96},{128,112},... | collective-permute-start | bytes 24584 | tf_op jit(solution)/shard_map/ppermute | solution.py:42
  203.9 4.5 %collective-permute-start.39 = (f32[10,1,128]{2,1,0:T(1,128)S(1)}, f32[10,1,128]{2,1,0:T(1,128)S(1)}, u32[]{:S(2)}, u32[]{:S(2)}) collective-permute-start(f32[10,1,128]{2,1,0:T(1,128)S(1)} %get-tuple-element.65), channel_id=1, source_target_pairs={{0,1},{1,2},{2,3},{3,4},{4,5},{5,6},{6,7},{7,8},{8,9},{9,10},{10,1... | collective-permute-start | bytes 15368 | tf_op jit(solution)/shard_map/ppermute | solution.py:41
  207.0 5.5 %collective-permute-start.38 = (f32[10,1,128]{2,1,0:T(1,128)S(1)}, f32[10,1,128]{2,1,0:T(1,128)S(1)}, u32[]{:S(2)}, u32[]{:S(2)}) collective-permute-start(f32[10,1,128]{2,1,0:T(1,128)S(1)} %get-tuple-element.66), channel_id=1, source_target_pairs={{1,0},{2,1},{3,2},{4,3},{5,4},{6,5},{7,6},{8,7},{9,8},{10,9},{11,1... | collective-permute-start | bytes 15368 | tf_op jit(solution)/shard_map/ppermute | solution.py:42
  212.9 7.7 %collective-permute-start.41 = (f32[1,16,128]{2,1,0:T(8,128)S(1)}, f32[1,16,128]{2,1,0:T(8,128)S(1)}, u32[]{:S(2)}, u32[]{:S(2)}) collective-permute-start(f32[1,16,128]{2,1,0:T(8,128)S(1)} %get-tuple-element.79), channel_id=1, source_target_pairs={{0,16},{16,32},{32,48},{48,64},{64,80},{80,96},{96,112},{112,128},... | collective-permute-start | bytes 24584 | tf_op jit(solution)/shard_map/ppermute | solution.py:41
  214.8 7.1 %collective-permute-start.40 = (f32[1,16,128]{2,1,0:T(8,128)S(1)}, f32[1,16,128]{2,1,0:T(8,128)S(1)}, u32[]{:S(2)}, u32[]{:S(2)}) collective-permute-start(f32[1,16,128]{2,1,0:T(8,128)S(1)} %get-tuple-element.80), channel_id=1, source_target_pairs={{16,0},{32,16},{48,32},{64,48},{80,64},{96,80},{112,96},{128,112},... | collective-permute-start | bytes 24584 | tf_op jit(solution)/shard_map/ppermute | solution.py:42
  221.9 4.5 %collective-permute-start.43 = (f32[10,1,128]{2,1,0:T(1,128)S(1)}, f32[10,1,128]{2,1,0:T(1,128)S(1)}, u32[]{:S(2)}, u32[]{:S(2)}) collective-permute-start(f32[10,1,128]{2,1,0:T(1,128)S(1)} %get-tuple-element.63), channel_id=1, source_target_pairs={{0,1},{1,2},{2,3},{3,4},{4,5},{5,6},{6,7},{7,8},{8,9},{9,10},{10,1... | collective-permute-start | bytes 15368 | tf_op jit(solution)/shard_map/ppermute | solution.py:41
  225.0 5.5 %collective-permute-start.42 = (f32[10,1,128]{2,1,0:T(1,128)S(1)}, f32[10,1,128]{2,1,0:T(1,128)S(1)}, u32[]{:S(2)}, u32[]{:S(2)}) collective-permute-start(f32[10,1,128]{2,1,0:T(1,128)S(1)} %get-tuple-element.64), channel_id=1, source_target_pairs={{1,0},{2,1},{3,2},{4,3},{5,4},{6,5},{7,6},{8,7},{9,8},{10,9},{11,1... | collective-permute-start | bytes 15368 | tf_op jit(solution)/shard_map/ppermute | solution.py:42
  (3 other events, 19.3 us)
where the time goes:
time: 233 us; the launch traced here: 231 us
  starting transfers between devices  143 us (61%)
  waiting for transfers between devices  65.6 us (28%)
  other arithmetic  18.6 us (8%)
  local copies, waits for them, and re-layouts  2.71 us (1%)
    ppermute x22, starting transfers between devices, padded_2(): after = lax.ppermute(leading, axis, down)  77.8 us
    ppermute x22, starting transfers between devices, padded_2(): before = lax.ppermute(last, axis, up)  64.9 us
    ppermute x22, waiting for transfers between devices, padded_2(): after = lax.ppermute(leading, axis, down)  61.1 us
    concatenate x21, other arithmetic, padded_2(): x = jnp.concatenate([before, x, after], axis=dim)  12.4 us
  transfers between devices with their start and end apart: 44, of which 28 were waited for; matrix products, arithmetic and copies ran while one was open for 1% of the time, Pallas kernels for 0%

commit v1 on v0

v1 whole, which is shorter than its diff:
```python
import math

import jax
import jax.numpy as jnp
from jax import lax
from jax.experimental import pallas as pl
from jax.experimental.pallas import tpu as pltpu
from jax.sharding import PartitionSpec as P

MESH = pl.DeviceIdType.MESH
SWEEPS = 8
VELOCITIES = (
    (0, 0, 0),
    (1, 0, 0),
    (-1, 0, 0),
    (0, 1, 0),
    (0, -1, 0),
    (0, 0, 1),
    (0, 0, -1),
    (1, 1, 0),
    (-1, -1, 0),
    (1, -1, 0),
    (-1, 1, 0),
    (1, 0, 1),
    (-1, 0, -1),
    (1, 0, -1),
    (-1, 0, 1),
    (0, 1, 1),
    (0, -1, -1),
    (0, 1, -1),
    (0, -1, 1),
)
DIRS = ((1, 0), (-1, 0), (0, 1), (0, -1), (1, 1), (1, -1), (-1, 1), (-1, -1))
NX, NY, NZ = 8, 16, 128
X0, XF, Y0 = 3, 8, 16
ROWS = 48
STEP_X, FILTER_X = NX + 2 * X0, NX + 2 * XF
def src_span(side, length, first, last):
    if side > 0:
        return pl.ds(length - last, last - first + 1)
    if side < 0:
        return pl.ds(first - 1, last - first + 1)
    return pl.ds(0, length)


def dst_span(side, length, own, first, last):
    if side > 0:
        return pl.ds(own - last, last - first + 1)
    if side < 0:
        return pl.ds(own + length + first - 1, last - first + 1)
    return pl.ds(own, length)


def planes(first, end, together, body):
    main = (end - first) // together * together

    if main > together:

        @pl.loop(first, first + main, step=together)
        def _(x):
            for j in range(together):
                body(x + j)

    else:
        main = 0
    for x in range(first + main, end):
        body(x)


def runs_of(sx, sy):
    runs = []
    for i, (cx, cy, _) in enumerate(VELOCITIES):
        depth = (2 - sx * cx, 2 - sy * cy)
        if runs and runs[-1][2] == depth:
            runs[-1] = (runs[-1][0], runs[-1][1] + 1, depth)
        else:
            runs.append((i, 1, depth))
    return runs


def rows_in(*parts):
    return sum(math.prod(p.shape) // NZ for p in parts)


def exchange_kernel(
    pop, vel, heat, obj, liq, span,
    state_out, sens, scale_out, gain_out,
    s0, s1, u0, obj0, liq0, span0, heat0, um, ka, kb, dsum, count,
    load_sem, ssem, rsem, ready,
):
    grp, blk = lax.axis_index("grp"), lax.axis_index("blk")
    n_grp, n_blk = lax.axis_size("grp"), lax.axis_size("blk")
    late = (grp == 0) & (blk == 0)

    def exists(d):
        ok = None
        for side, at, n in ((d[0], grp, n_grp), (d[1], blk, n_blk)):
            if side:
                one = at < n - 1 if side > 0 else at > 0
                ok = one if ok is None else ok & one
        return ok

    def to_late(d):
        return (grp + d[0] == 0) & (blk + d[1] == 0)

    def opposite(d):
        return (-d[0], -d[1])

    def peer(d):
        return dict(device_id=(grp + d[0], blk + d[1]), device_id_type=MESH)

    def remote(d, j, src, dst):
        k = DIRS.index(d)
        return pltpu.make_async_remote_copy(
            src_ref=src, dst_ref=dst, send_sem=ssem.at[j, k], recv_sem=rsem.at[j, k], **peer(d)
        )

    def part(d, src, dst, lead, depth, own_x):
        xs, ys = src_span(d[0], NX, 1, depth[0]), src_span(d[1], NY, 1, depth[1])
        xd = dst_span(d[0], NX, own_x, 1, depth[0])
        yd = dst_span(d[1], NY, Y0, 1, depth[1])
        return src.at[lead + (xs, ys)], dst.at[lead + (xd, yd)]

    def state_parts(d):
        parts = [part(d, pop, s0, (pl.ds(a, n),), depth, X0) for a, n, depth in runs_of(*d)]
        parts.append(part(d, vel, u0, (pl.ds(0, 3),), (2, 2), X0))
        parts.append(part(d, obj, obj0, (), (2, 2), X0))
        parts.append(part(d, liq, liq0, (), (2, 2), X0))
        return parts

    def filter_pieces(d):
        dx, dy = d
        if dx and dy:
            near = ((1, 3, 1, 7), (4, 7, 1, 4))
        else:
            near = ((1, XF, 1, XF),)
        return [
            (src_span(dx, NX, a, b), src_span(dy, NY, c, e),
             dst_span(dx, NX, XF, a, b), dst_span(dy, NY, Y0, c, e))
            for a, b, c, e in near
        ]

    def span_parts(d):
        return [(span.at[xs, ys], span0.at[xd, yd]) for xs, ys, xd, yd in filter_pieces(d)]

    def sens_parts(d):
        return [
            (sens.at[pl.ds(xs.start + XF, xs.size), pl.ds(ys.start + Y0, ys.size)], sens.at[xd, yd])
            for xs, ys, xd, yd in filter_pieces(d)
        ]

    stages = (state_parts, span_parts, sens_parts)

    def send(j, d):
        for src, dst in stages[j](d):
            remote(d, j, src, dst).start()

    def whole(j, d):
        rows = count.at[pl.ds(0, rows_in(*(src for src, _ in stages[j](d))))]
        return remote(d, j, rows, rows)

    def wait_recv(j):
        for d in DIRS:
            pl.when(exists(opposite(d)))(lambda d=d: whole(j, d).wait_recv())

    barrier = pltpu.get_barrier_semaphore()
    expected = 0
    for d in DIRS:
        pl.when(exists(d) & ~late)(lambda d=d: pl.semaphore_signal(barrier, inc=1, **peer(d)))
        expected += jnp.where(exists(d) & ~to_late(d), 1, 0)
    pl.semaphore_wait(barrier, expected)

    @pl.when(late)
    def _():
        for d in ((0, 1), (1, 1), (1, 0)):
            pl.semaphore_signal(ready, inc=1, **peer(d))

    order = ((0, 1), (0, -1), (1, 0), (-1, 0), (1, 1), (1, -1), (-1, 1), (-1, -1))
    for d in order:
        pl.when(exists(d) & ~to_late(d))(lambda d=d: send(0, d))

    own = (pl.ds(X0, NX), pl.ds(Y0, NY))
    loads = [
        pltpu.make_async_copy(src, dst, load_sem.at[j])
        for j, (src, dst) in enumerate(
            (
                (pop, s0.at[(pl.ds(0, 19),) + own]),
                (vel, u0.at[(pl.ds(0, 3),) + own]),
                (obj, obj0.at[own]),
                (liq, liq0.at[own]),
                (heat, heat0),
                (span, span0.at[pl.ds(XF, NX), pl.ds(Y0, NY)]),
            )
        )
    ]
    for c in loads:
        c.start()
    for d in order:
        pl.when(exists(d) & ~to_late(d))(lambda d=d: send(1, d))

    def outside(x_step, x_filter, rows):
        def fill(first, count, width, put):
            @pl.loop(first, first + count)
            def _(x):
                for r in rows:
                    put(x, pl.ds(r, 8))

        zero = jnp.zeros((8, NZ), jnp.float32)
        none = jnp.full((8, NZ), -1, jnp.int32)

        def put_step(x, r):
            for i in range(19):
                s0[i, x, r] = zero
            for i in range(3):
                u0[i, x, r] = zero
            obj0[x, r] = zero
            liq0[x, r] = none

        def put_filter(x, r):
            span0[x, r] = none
            sens[x, r] = zero

        fill(*x_step, None, put_step)
        fill(*x_filter, None, put_filter)

    groups = (8, 16, 24, 32)
    pl.when(grp == 0)(lambda: outside((0, X0), (0, XF), groups))
    pl.when(grp == n_grp - 1)(lambda: outside((X0 + NX, X0), (XF + NX, XF), groups))
    pl.when(blk == 0)(lambda: outside((0, STEP_X), (0, FILTER_X), (8,)))
    pl.when(blk == n_blk - 1)(lambda: outside((0, STEP_X), (0, FILTER_X), (32,)))

    for d in ((0, -1), (-1, -1), (-1, 0)):

        @pl.when(exists(d) & to_late(d))
        def _():
            pl.semaphore_wait(ready, 1)
            send(0, d)
            send(1, d)

    for c in loads:
        c.wait()
    wait_recv(0)

    lane = lax.broadcasted_iota(jnp.int32, (8, NZ), 1)

    def step(number, src, x, r0):
        def pulled(i):
            cx, cy, cz = VELOCITIES[i]
            v = src[i, x + cx, pl.ds(r0 + cy, 8)]
            if cz > 0:
                return jnp.where(lane == NZ - 1, 0.0, pltpu.roll(v, NZ - 1, 1))
            if cz < 0:
                return jnp.where(lane == 0, 0.0, pltpu.roll(v, 1, 1))
            return v

        p = [pulled(i) for i in range(19)]
        rows = pl.ds(r0, 8)
        if number == 0:
            kind = liq0[x, rows]
            fluid = kind.astype(jnp.float32)
            inside = kind >= 0
            omega = 0.9 + 0.7 * fluid
            b = jnp.where(inside, omega, 0.0)
            a = jnp.where(inside, 1.0 - omega, 0.0)
            third = fluid * (3.0 / 36.0)
            ux, uy, uz = (u0[i, x, rows] * third for i in range(3))
            ka[x, rows] = a
            kb[x, rows] = b
            um[0, x, rows] = ux
            um[1, x, rows] = uy
            um[2, x, rows] = uz
        else:
            a, b = ka[x, rows], kb[x, rows]
            ux, uy, uz = (um[i, x, rows] for i in range(3))
        total = {i: p[i] + p[i + 1] for i in range(1, 19, 2)}
        diff = {i: p[i] - p[i + 1] for i in range(1, 19, 2)}
        faces = total[1] + total[3] + total[5]
        edges = (total[7] + total[9]) + (total[11] + total[13]) + (total[15] + total[17])
        average = p[0] * (1.0 / 3.0) + faces * (1.0 / 18.0) + edges * (1.0 / 36.0)
        mx = (diff[1] + diff[1]) + (diff[7] + diff[9]) + (diff[11] + diff[13])
        my = (diff[3] + diff[3]) + (diff[7] - diff[9]) + (diff[15] + diff[17])
        mz = (diff[5] + diff[5]) + (diff[11] - diff[13]) + (diff[15] - diff[17])
        extra = ux * mx + uy * my + uz * mz
        pushed = b * (average + extra)
        o = obj0[x, rows] * (1.0 / 36.0)
        o2 = o + o
        adds = (pushed + 12.0 * o, pushed + o2, pushed + o)
        return [a * p[i] + adds[0 if i == 0 else 1 if i < 7 else 2] for i in range(19)], extra

    def step_1(x):
        for r0 in groups:
            posts, extra = step(0, s0, x, r0)
            for i in range(19):
                s1[i, x, pl.ds(r0, 8)] = posts[i]
            if r0 in (16, 24):
                dsum[x, pl.ds(r0, 8)] = extra

    planes(1, STEP_X - 1, 2, step_1)

    def step_2(x):
        for r0 in groups:
            posts, extra = step(1, s1, x, r0)
            for i in range(19):
                s0[i, x, pl.ds(r0, 8)] = posts[i]
            if r0 in (16, 24):
                dsum[x, pl.ds(r0, 8)] += extra

    planes(2, STEP_X - 2, 2, step_2)

    def step_3(x):
        for r0 in (16, 24):
            posts, extra = step(2, s0, x, r0)
            for i in range(19):
                state_out[i, x - X0, pl.ds(r0 - Y0, 8)] = posts[i]
            total = dsum[x, pl.ds(r0, 8)] + extra
            sens[x - X0 + XF, pl.ds(r0, 8)] = heat0[x - X0, pl.ds(r0 - Y0, 8)] * total

    planes(3, STEP_X - 3, 4, step_3)

    for d in order:
        pl.when(exists(d))(lambda d=d: send(2, d))

    wait_recv(1)

    def weigh(x):
        for r0 in groups:
            rows = pl.ds(r0, 8)
            k = span0[x, rows]
            r2 = jnp.where(k == 0, 0.25, jnp.where(k == 1, 1.0, jnp.where(k == 2, 4.0, 16.0)))
            gain = jnp.where(k >= 0, 1.0 / (1.0 + 6.0 * r2), 0.0)
            gain_out[x, rows] = gain
            scale_out[x, rows] = gain * r2

    planes(0, FILTER_X, 4, weigh)

    wait_recv(2)
    for d in DIRS:

        @pl.when(exists(d))
        def _():
            for j in range(3):
                whole(j, d).wait_send()


def sweep_kernel(state, sens, scale, gain, state_out, smooth_out, own, q0, q1, sem):
    copy = pltpu.make_async_copy(state, state_out, sem)
    copy.start()
    lane = lax.broadcasted_iota(jnp.int32, (8, NZ), 1)
    for number in range(1, SWEEPS + 1):
        last = number == SWEEPS
        src = sens if number == 1 else (q0 if number % 2 == 0 else q1)
        dst = q0 if number % 2 == 1 else q1
        groups = (16, 24) if last else (8, 16, 24, 32)

        def sweep(x):
            for r0 in groups:
                rows = pl.ds(r0, 8)
                mid = src[x, rows]
                beside = src[x - 1, rows] + src[x + 1, rows]
                beside += src[x, pl.ds(r0 - 1, 8)] + src[x, pl.ds(r0 + 1, 8)]
                beside += jnp.where(lane == NZ - 1, 0.0, pltpu.roll(mid, NZ - 1, 1))
                beside += jnp.where(lane == 0, 0.0, pltpu.roll(mid, 1, 1))
                if number == 1:
                    base = mid * gain[x, rows]
                    own[x, rows] = base
                else:
                    base = own[x, rows]
                value = base + scale[x, rows] * beside
                if last:
                    smooth_out[x - XF, pl.ds(r0 - Y0, 8)] = value
                else:
                    dst[x, rows] = value

        planes(number, FILTER_X - number, FILTER_X, sweep)

    copy.wait()


def on_device(pop, vel, heat, obj, liq, span):
    f32, i32 = jnp.float32, jnp.int32
    vmem = pl.BlockSpec(memory_space=pltpu.VMEM)
    anywhere = pl.BlockSpec(memory_space=pltpu.HBM)
    frame = (FILTER_X, ROWS, NZ)
    step_frame = (STEP_X, ROWS, NZ)
    args = [
        pltpu.with_memory_space_constraint(x, pltpu.HBM)
        for x in (pop, vel, heat, obj, liq, span)
    ]
    state, sens, scale, gain = pl.pallas_call(
        exchange_kernel,
        out_shape=(
            jax.ShapeDtypeStruct((19, NX, NY, NZ), f32),
            jax.ShapeDtypeStruct(frame, f32),
            jax.ShapeDtypeStruct(frame, f32),
            jax.ShapeDtypeStruct(frame, f32),
        ),
        in_specs=[anywhere] * 6,
        out_specs=(vmem,) * 4,
        scratch_shapes=[
            pltpu.VMEM((19,) + step_frame, f32),
            pltpu.VMEM((19,) + step_frame, f32),
            pltpu.VMEM((3,) + step_frame, f32),
            pltpu.VMEM(step_frame, f32),
            pltpu.VMEM(step_frame, i32),
            pltpu.VMEM(frame, i32),
            pltpu.VMEM((NX, NY, NZ), f32),
            pltpu.VMEM((3,) + step_frame, f32),
            pltpu.VMEM(step_frame, f32),
            pltpu.VMEM(step_frame, f32),
            pltpu.VMEM(step_frame, f32),
            pltpu.VMEM((1024, NZ), f32),
            pltpu.SemaphoreType.DMA((6,)),
            pltpu.SemaphoreType.DMA((3, 8)),
            pltpu.SemaphoreType.DMA((3, 8)),
            pltpu.SemaphoreType.REGULAR,
        ],
        compiler_params=pltpu.CompilerParams(
            collective_id=0, has_side_effects=True, vmem_limit_bytes=36 << 20
        ),
        name="steps",
    )(*args)
    return pl.pallas_call(
        sweep_kernel,
        out_shape=(
            jax.ShapeDtypeStruct((19, NX, NY, NZ), f32),
            jax.ShapeDtypeStruct((NX, NY, NZ), f32),
        ),
        in_specs=[vmem] * 4,
        out_specs=(anywhere, vmem),
        scratch_shapes=[
            pltpu.VMEM(frame, f32),
            pltpu.VMEM(frame, f32),
            pltpu.VMEM(frame, f32),
            pltpu.SemaphoreType.DMA,
        ],
        compiler_params=pltpu.CompilerParams(vmem_limit_bytes=36 << 20),
        name="sweeps",
    )(state, sens, scale, gain)


def solution(mesh):
    field = P("grp", "blk", None)
    many = P(None, "grp", "blk", None)
    return jax.shard_map(
        on_device,
        mesh=mesh,
        in_specs=(many, many, field, field, field, field),
        out_specs=(many, field),
        check_vma=False,
    )
```

time: 233 us -> 27 us (0.12)
  the two profiles are of different devices: /device:TPU:6 before, /device:TPU:102 now
where the time goes in v1:
time: 27 us; the launch traced here: 26.9 us
  Pallas kernels  26.2 us (97%)
  between operations  0.64 us (2%)
    pallas_call x1, Pallas kernels, on_device(): pl.pallas_call(exchange_kernel, out_shape=(jax.ShapeDtypeStruct((19, NX,...  24.5 us
    pallas_call x1, Pallas kernels, on_device(): pl.pallas_call(sweep_kernel, out_shape=(jax.ShapeDtypeStruct((19, NX, NY,...  1.72 us

profile of v1, /device:TPU:102, one launch (start us, length us, event | category | flops | bytes accessed | tf_op | source)
XLA Modules:
  0.0 26.9 jit_solution(14718613897752336993)
XLA Ops:
  0.6 24.5 %steps.1 = (f32[19,8,16,128]{3,2,1,0:T(8,128)S(1)}, f32[24,48,128]{2,1,0:T(8,128)S(1)}, f32[24,48,128]{2,1,0:T(8,128)S(1)}, f32[24,48,128]{2,1,0:T(8,128)S(1)}) custom-call(f32[19,8,16,128]{3,2,1,0:T(8,128)} %pop.1, f32[3,8,16,128]{3,2,1,0:T(8,128)} %vel.1, f32[8,16,128]{2,1,0:T(8,128)} %heat.1, f32[8,16,128]{2,1,0:T(8,128)} %obj.1, s32[8,16,128]{2,1,0:T(8,128)} %liq.1, ...), custom_call_target="tpu_custom_call" | custom-call | tf_op jit(solution)/shard_map/steps/pallas_call | solution.py:389
  25.1 1.7 %sweeps.1 = (f32[19,8,16,128]{3,2,1,0:T(8,128)}, f32[8,16,128]{2,1,0:T(8,128)}) custom-call(f32[19,8,16,128]{3,2,1,0:T(8,128)S(1)} %get-tuple-element.6.state, f32[24,48,128]{2,1,0:T(8,128)S(1)} %get-tuple-element.7.sens, f32[24,48,128]{2,1,0:T(8,128)S(1)} %get-tuple-element.8.scale, f32[24,48,128]{2,1,0:T(8,128)S(1)} %get-tuple-element.9.gain), custom_call_target="tpu_custom_call" | custom-call | tf_op jit(solution)/shard_map/sweeps/pallas_call | solution.py:422

commit v2 on v1

--- a/solution.py
+++ b/solution.py
@@ -1,3 +1,4 @@
+import functools
 import math
 
 import jax
@@ -85,13 +86,11 @@
 def exchange_kernel(
     pop, vel, heat, obj, liq, span,
     state_out, sens, scale_out, gain_out,
-    s0, s1, u0, obj0, liq0, span0, heat0, um, ka, kb, dsum, count,
+    s0, s1, u0, obj0, liq0, span0, heat0, um, ka, kb, extras, count,
     load_sem, ssem, rsem, ready,
 ):
     grp, blk = lax.axis_index("grp"), lax.axis_index("blk")
     n_grp, n_blk = lax.axis_size("grp"), lax.axis_size("blk")
-    late = (grp == 0) & (blk == 0)
-
     def exists(d):
         ok = None
         for side, at, n in ((d[0], grp, n_grp), (d[1], blk, n_blk)):
@@ -100,8 +99,23 @@
                 ok = one if ok is None else ok & one
         return ok
 
-    def to_late(d):
+    def origin(d):
         return (grp + d[0] == 0) & (blk + d[1] == 0)
+
+    def mutual(d):
+        return ~origin((0, 0)) & ~origin(d)
+
+    def first(d):
+        if d[1] > 0:
+            later = ~origin((0, 0))
+        elif d[1] < 0:
+            later = origin(d)
+        else:
+            later = origin(d) | (~origin((0, 0)) & (grp % 2 == 1))
+        return later & ~mutual(d)
+
+    def ahead(d):
+        return exists(d) & ~first(d)
 
     def opposite(d):
         return (-d[0], -d[1])
@@ -111,22 +125,56 @@
 
     def remote(d, j, src, dst):
         k = DIRS.index(d)
+        to = peer((d[0], 0)) if j == PASSED else peer(d)
         return pltpu.make_async_remote_copy(
-            src_ref=src, dst_ref=dst, send_sem=ssem.at[j, k], recv_sem=rsem.at[j, k], **peer(d)
+            src_ref=src, dst_ref=dst, send_sem=ssem.at[j, k], recv_sem=rsem.at[j, k], **to
         )
 
-    def part(d, src, dst, lead, depth, own_x):
+    def part(d, src, dst, lead, depth, own_x, cut=None):
         xs, ys = src_span(d[0], NX, 1, depth[0]), src_span(d[1], NY, 1, depth[1])
         xd = dst_span(d[0], NX, own_x, 1, depth[0])
         yd = dst_span(d[1], NY, Y0, 1, depth[1])
+        if cut:
+            xs, xd = pl.ds(cut[0], cut[1]), pl.ds(own_x + cut[0], cut[1])
         return src.at[lead + (xs, ys)], dst.at[lead + (xd, yd)]
 
-    def state_parts(d):
-        parts = [part(d, pop, s0, (pl.ds(a, n),), depth, X0) for a, n, depth in runs_of(*d)]
-        parts.append(part(d, vel, u0, (pl.ds(0, 3),), (2, 2), X0))
-        parts.append(part(d, obj, obj0, (), (2, 2), X0))
-        parts.append(part(d, liq, liq0, (), (2, 2), X0))
+    def state_parts(d, cut):
+        parts = [part(d, pop, s0, (pl.ds(a, n),), depth, X0, cut) for a, n, depth in runs_of(*d)]
+        parts.append(part(d, vel, u0, (pl.ds(0, 3),), (2, 2), X0, cut))
+        parts.append(part(d, obj, obj0, (), (2, 2), X0, cut))
+        parts.append(part(d, liq, liq0, (), (2, 2), X0, cut))
         return parts
+
+    even = grp % 2 == 0
+
+    def rim_parts(d):
+        return state_parts(d, None if d[0] else (jnp.where(even, 0, 3), NX - 3))
+
+    def near_parts(d):
+        return state_parts(d, (jnp.where(even, NX - 3, 0), 3))
+
+    def passed_parts(d):
+        dx, dy = d
+        parts = []
+
+        def add(frame, lead, depth):
+            rows = dst_span(dy, NY, Y0, 1, depth[1])
+            xs = src_span(dx, NX, 1, depth[0])
+            xs, xd = pl.ds(X0 + xs.start, xs.size), dst_span(dx, NX, X0, 1, depth[0])
+            parts.append((frame.at[lead + (xs, rows)], frame.at[lead + (xd, rows)]))
+
+        for a, n, depth in runs_of(*d):
+            add(s0, (pl.ds(a, n),), depth)
+        add(u0, (pl.ds(0, 3),), (2, 2))
+        add(obj0, (), (2, 2))
+        add(liq0, (), (2, 2))
+        return parts
+
+    def direct(d):
+        return (even if d[0] < 0 else ~even) if d[0] and d[1] else True
+
+    def passes(d):
+        return exists((0, -d[1])) & ~direct(d)
 
     def filter_pieces(d):
         dx, dy = d
@@ -144,40 +192,75 @@
         return [(span.at[xs, ys], span0.at[xd, yd]) for xs, ys, xd, yd in filter_pieces(d)]
 
     def sens_parts(d):
+        pieces = filter_pieces(d)
+        if not d[1]:
+            xs, _, xd, _ = pieces[0]
+            halves = (0, NY // 2), (NY // 2, NY // 2)
+            pieces = [(xs, pl.ds(a, n), xd, pl.ds(Y0 + a, n)) for a, n in halves]
         return [
             (sens.at[pl.ds(xs.start + XF, xs.size), pl.ds(ys.start + Y0, ys.size)], sens.at[xd, yd])
-            for xs, ys, xd, yd in filter_pieces(d)
+            for xs, ys, xd, yd in pieces
         ]
 
-    stages = (state_parts, span_parts, sens_parts)
-
-    def send(j, d):
-        for src, dst in stages[j](d):
-            remote(d, j, src, dst).start()
+    RIM, SPAN, SENS, NEAR, PASSED = range(5)
+    stages = (rim_parts, span_parts, sens_parts, near_parts, passed_parts)
 
     def whole(j, d):
         rows = count.at[pl.ds(0, rows_in(*(src for src, _ in stages[j](d))))]
         return remote(d, j, rows, rows)
 
+    def send(j, d, half=0):
+        parts = stages[j](d)
+        if j == SENS and not d[1]:
+            parts = parts[half : half + 1]
+        for src, dst in parts:
+            remote(d, j, src, dst).start()
+
+    def sends(j, d):
+        return passes(d) if j == PASSED else exists(d) & direct(d) if j == RIM else exists(d)
+
+    def gets(j, d):
+        if j == PASSED:
+            return exists((0, -d[1])) & direct(d)
+        if j == RIM and d[0] and d[1]:
+            return exists(opposite(d)) & ~direct(d)
+        return exists(opposite(d))
+
+    def directions(j):
+        if j == NEAR:
+            return ((0, 1), (0, -1))
+        if j == PASSED:
+            return ((1, 1), (1, -1), (-1, 1), (-1, -1))
+        return DIRS
+
     def wait_recv(j):
-        for d in DIRS:
-            pl.when(exists(opposite(d)))(lambda d=d: whole(j, d).wait_recv())
+        for d in directions(j):
+            pl.when(gets(j, d))(lambda d=d: whole(j, d).wait_recv())
+
+    def wait_send(j):
+        for d in directions(j):
+            pl.when(sends(j, d))(lambda d=d: whole(j, d).wait_send())
 
     barrier = pltpu.get_barrier_semaphore()
     expected = 0
     for d in DIRS:
-        pl.when(exists(d) & ~late)(lambda d=d: pl.semaphore_signal(barrier, inc=1, **peer(d)))
-        expected += jnp.where(exists(d) & ~to_late(d), 1, 0)
-    pl.semaphore_wait(barrier, expected)
-
-    @pl.when(late)
-    def _():
-        for d in ((0, 1), (1, 1), (1, 0)):
-            pl.semaphore_signal(ready, inc=1, **peer(d))
-
-    order = ((0, 1), (0, -1), (1, 0), (-1, 0), (1, 1), (1, -1), (-1, 1), (-1, -1))
+        before = exists(d) & (first(d) | mutual(d))
+        pl.when(before)(lambda d=d: pl.semaphore_signal(barrier, inc=1, **peer(d)))
+        expected += jnp.where(ahead(d), 1, 0)
+    pl.when(expected > 0)(lambda: pl.semaphore_wait(barrier, expected))
+
+    corners = ((1, 1), (1, -1), (-1, 1), (-1, -1))
+    order = corners + ((1, 0), (-1, 0), (0, 1), (0, -1))
+    work = [(RIM, d) for d in order[4:6] + corners] + [(NEAR, (0, 1)), (NEAR, (0, -1))]
+    work += [(RIM, d) for d in order[6:]]
+
+    def greet(d):
+        pl.semaphore_signal(ready.at[DIRS.index(d)], inc=1, **peer(d))
+
     for d in order:
-        pl.when(exists(d) & ~to_late(d))(lambda d=d: send(0, d))
+        pl.when(ahead(d) & ~mutual(d))(lambda d=d: greet(d))
+    for j, d in work:
+        pl.when(ahead(d) & sends(j, d))(lambda j=j, d=d: send(j, d))
 
     own = (pl.ds(X0, NX), pl.ds(Y0, NY))
     loads = [
@@ -195,8 +278,15 @@
     ]
     for c in loads:
         c.start()
-    for d in order:
-        pl.when(exists(d) & ~to_late(d))(lambda d=d: send(1, d))
+
+    for d in ((1, 0), (-1, 0), (1, 1), (-1, 1), (0, 1), (0, -1), (-1, -1)):
+
+        @pl.when(exists(d) & first(d))
+        def _():
+            pl.semaphore_wait(ready.at[DIRS.index(opposite(d))], 1)
+            for j, to in work:
+                if to == d:
+                    pl.when(sends(j, d))(lambda j=j, d=d: send(j, d))
 
     def outside(x_step, x_filter, rows):
         def fill(first, count, width, put):
@@ -229,18 +319,13 @@
     pl.when(blk == 0)(lambda: outside((0, STEP_X), (0, FILTER_X), (8,)))
     pl.when(blk == n_blk - 1)(lambda: outside((0, STEP_X), (0, FILTER_X), (32,)))
 
-    for d in ((0, -1), (-1, -1), (-1, 0)):
-
-        @pl.when(exists(d) & to_late(d))
-        def _():
-            pl.semaphore_wait(ready, 1)
-            send(0, d)
-            send(1, d)
-
+    wait_recv(NEAR)
+    for d in corners:
+        pl.when(passes(d))(lambda d=d: send(PASSED, d))
+    for d in order:
+        pl.when(exists(d))(lambda d=d: send(SPAN, d))
     for c in loads:
         c.wait()
-    wait_recv(0)
-
     lane = lax.broadcasted_iota(jnp.int32, (8, NZ), 1)
 
     def step(number, src, x, r0):
@@ -287,40 +372,49 @@
         adds = (pushed + 12.0 * o, pushed + o2, pushed + o)
         return [a * p[i] + adds[0 if i == 0 else 1 if i < 7 else 2] for i in range(19)], extra
 
-    def step_1(x):
-        for r0 in groups:
+    def step_1(starts, x):
+        for r0 in starts:
+            rows = pl.ds(r0, 8)
             posts, extra = step(0, s0, x, r0)
             for i in range(19):
-                s1[i, x, pl.ds(r0, 8)] = posts[i]
-            if r0 in (16, 24):
-                dsum[x, pl.ds(r0, 8)] = extra
-
-    planes(1, STEP_X - 1, 2, step_1)
-
-    def step_2(x):
-        for r0 in groups:
+                s1[i, x, rows] = posts[i]
+            extras[0, x, rows] = extra
+
+    def step_2(starts, x):
+        for r0 in starts:
+            rows = pl.ds(r0, 8)
             posts, extra = step(1, s1, x, r0)
             for i in range(19):
-                s0[i, x, pl.ds(r0, 8)] = posts[i]
-            if r0 in (16, 24):
-                dsum[x, pl.ds(r0, 8)] += extra
-
-    planes(2, STEP_X - 2, 2, step_2)
-
-    def step_3(x):
-        for r0 in (16, 24):
+                s0[i, x, rows] = posts[i]
+            extras[1, x, rows] = extra
+
+    def step_3(starts, x):
+        for r0 in starts:
+            rows, here = pl.ds(r0, 8), pl.ds(r0 - Y0, 8)
             posts, extra = step(2, s0, x, r0)
             for i in range(19):
-                state_out[i, x - X0, pl.ds(r0 - Y0, 8)] = posts[i]
-            total = dsum[x, pl.ds(r0, 8)] + extra
-            sens[x - X0 + XF, pl.ds(r0, 8)] = heat0[x - X0, pl.ds(r0 - Y0, 8)] * total
-
-    planes(3, STEP_X - 3, 4, step_3)
-
-    for d in order:
-        pl.when(exists(d))(lambda d=d: send(2, d))
-
-    wait_recv(1)
+                state_out[i, x - X0, here] = posts[i]
+            total = extras[0, x, rows] + extras[1, x, rows] + extra
+            sens[x - X0 + XF, rows] = heat0[x - X0, here] * total
+
+    for side in (1, -1):
+        low = side > 0
+        for j in (RIM, PASSED):
+            for d in directions(j):
+                if d[1] == side or (low and d[1] == 0):
+                    pl.when(gets(j, d))(lambda j=j, d=d: whole(j, d).wait_recv())
+        starts = ((Y0 - 2, Y0 + 2), (Y0 - 1, Y0 + 1), (Y0,)) if low else ((Y0 + 10,), (Y0 + 9,), (Y0 + 8,))
+        planes(1, STEP_X - 1, 4 if low else 6, functools.partial(step_1, starts[0]))
+        for d in corners:
+            if d[1] == side:
+                pl.when(sends(PASSED, d))(lambda d=d: whole(PASSED, d).wait_send())
+        planes(2, STEP_X - 2, 5, functools.partial(step_2, starts[1]))
+        planes(3, STEP_X - 3, 8, functools.partial(step_3, starts[2]))
+        for d in order:
+            if d[1] in (0, -side):
+                pl.when(exists(d))(lambda d=d: send(SENS, d, 0 if low else 1))
+
+    wait_recv(SPAN)
 
     def weigh(x):
         for r0 in groups:
@@ -333,27 +427,27 @@
 
     planes(0, FILTER_X, 4, weigh)
 
-    wait_recv(2)
-    for d in DIRS:
-
-        @pl.when(exists(d))
-        def _():
-            for j in range(3):
-                whole(j, d).wait_send()
-
-
-def sweep_kernel(state, sens, scale, gain, state_out, smooth_out, own, q0, q1, sem):
-    copy = pltpu.make_async_copy(state, state_out, sem)
-    copy.start()
+    wait_recv(SENS)
+    for j in (RIM, SPAN, SENS, NEAR):
+        wait_send(j)
+
+
+def sweep_kernel(state, sens, scale, gain, state_out, smooth_out, own, q0, q1, smooth, sem):
+    copies = (
+        pltpu.make_async_copy(state, state_out, sem.at[0]),
+        pltpu.make_async_copy(smooth, smooth_out, sem.at[1]),
+    )
+    copies[0].start()
     lane = lax.broadcasted_iota(jnp.int32, (8, NZ), 1)
     for number in range(1, SWEEPS + 1):
         last = number == SWEEPS
         src = sens if number == 1 else (q0 if number % 2 == 0 else q1)
         dst = q0 if number % 2 == 1 else q1
-        groups = (16, 24) if last else (8, 16, 24, 32)
-
-        def sweep(x):
-            for r0 in groups:
+        reach = SWEEPS - number
+        for x in range(number, FILTER_X - number):
+            over = max(XF - x, x - XF - NX + 1, 0)
+            low, high = Y0 - (reach - over), Y0 + NY + (reach - over)
+            for r0 in list(range(low, high - 8, 8)) + [high - 8]:
                 rows = pl.ds(r0, 8)
                 mid = src[x, rows]
                 beside = src[x - 1, rows] + src[x + 1, rows]
@@ -367,13 +461,13 @@
                     base = own[x, rows]
                 value = base + scale[x, rows] * beside
                 if last:
-                    smooth_out[x - XF, pl.ds(r0 - Y0, 8)] = value
+                    smooth[x - XF, pl.ds(r0 - Y0, 8)] = value
                 else:
                     dst[x, rows] = value
 
-        planes(number, FILTER_X - number, FILTER_X, sweep)
-
-    copy.wait()
+    copies[1].start()
+    for c in copies:
+        c.wait()
 
 
 def on_device(pop, vel, heat, obj, liq, span):
@@ -407,12 +501,12 @@
             pltpu.VMEM((3,) + step_frame, f32),
             pltpu.VMEM(step_frame, f32),
             pltpu.VMEM(step_frame, f32),
-            pltpu.VMEM(step_frame, f32),
+            pltpu.VMEM((2,) + step_frame, f32),
             pltpu.VMEM((1024, NZ), f32),
             pltpu.SemaphoreType.DMA((6,)),
-            pltpu.SemaphoreType.DMA((3, 8)),
-            pltpu.SemaphoreType.DMA((3, 8)),
-            pltpu.SemaphoreType.REGULAR,
+            pltpu.SemaphoreType.DMA((5, 8)),
+            pltpu.SemaphoreType.DMA((5, 8)),
+            pltpu.SemaphoreType.REGULAR((8,)),
         ],
         compiler_params=pltpu.CompilerParams(
             collective_id=0, has_side_effects=True, vmem_limit_bytes=36 << 20
@@ -426,12 +520,13 @@
             jax.ShapeDtypeStruct((NX, NY, NZ), f32),
         ),
         in_specs=[vmem] * 4,
-        out_specs=(anywhere, vmem),
+        out_specs=(anywhere, anywhere),
         scratch_shapes=[
             pltpu.VMEM(frame, f32),
             pltpu.VMEM(frame, f32),
             pltpu.VMEM(frame, f32),
-            pltpu.SemaphoreType.DMA,
+            pltpu.VMEM((NX, NY, NZ), f32),
+            pltpu.SemaphoreType.DMA((2,)),
         ],
         compiler_params=pltpu.CompilerParams(vmem_limit_bytes=36 << 20),
         name="sweeps",

time: 27 us -> 24.2 us (0.90)
  Pallas kernels: 26.2 us -> 23.4 us
    pallas_call x1, Pallas kernels: 24.5 us -> 21.8 us  [on_device(): pl.pallas_call(exchange_kernel, out_shape=(jax.ShapeDtypeStruct((19, NX,...]
where the time goes in v2:
time: 24.2 us; the launch traced here: 24.1 us
  Pallas kernels  23.4 us (97%)
  between operations  0.64 us (3%)
    pallas_call x1, Pallas kernels, on_device(): pl.pallas_call(exchange_kernel, out_shape=(jax.ShapeDtypeStruct((19, NX,...  21.8 us
    pallas_call x1, Pallas kernels, on_device(): pl.pallas_call(sweep_kernel, out_shape=(jax.ShapeDtypeStruct((19, NX, NY,...  1.66 us

profile of v2, /device:TPU:102, one launch (start us, length us, event | category | flops | bytes accessed | tf_op | source)
XLA Modules:
  0.0 24.1 jit_solution(2413864096001583878)
XLA Ops:
  0.6 21.8 %steps.1 = (f32[19,8,16,128]{3,2,1,0:T(8,128)S(1)}, f32[24,48,128]{2,1,0:T(8,128)S(1)}, f32[24,48,128]{2,1,0:T(8,128)S(1)}, f32[24,48,128]{2,1,0:T(8,128)S(1)}) custom-call(f32[19,8,16,128]{3,2,1,0:T(8,128)} %pop.1, f32[3,8,16,128]{3,2,1,0:T(8,128)} %vel.1, f32[8,16,128]{2,1,0:T(8,128)} %heat.1, f32[8,16,128]{2,1,0:T(8,128)} %obj.1, s32[8,16,128]{2,1,0:T(8,128)} %liq.1, ...), custom_call_target="tpu_custom_call" | custom-call | tf_op jit(solution)/shard_map/steps/pallas_call | solution.py:483
  22.4 1.7 %sweeps.1 = (f32[19,8,16,128]{3,2,1,0:T(8,128)}, f32[8,16,128]{2,1,0:T(8,128)}) custom-call(f32[19,8,16,128]{3,2,1,0:T(8,128)S(1)} %get-tuple-element.6.state, f32[24,48,128]{2,1,0:T(8,128)S(1)} %get-tuple-element.7.sens, f32[24,48,128]{2,1,0:T(8,128)S(1)} %get-tuple-element.8.scale, f32[24,48,128]{2,1,0:T(8,128)S(1)} %get-tuple-element.9.gain), custom_call_target="tpu_custom_call" | custom-call | tf_op jit(solution)/shard_map/sweeps/pallas_call | solution.py:516

commit v3 on v2

--- a/solution.py
+++ b/solution.py
@@ -35,6 +35,7 @@
 NX, NY, NZ = 8, 16, 128
 X0, XF, Y0 = 3, 8, 16
 ROWS = 48
+LOW_ROWS = 11
 STEP_X, FILTER_X = NX + 2 * X0, NX + 2 * XF
 def src_span(side, length, first, last):
     if side > 0:
@@ -130,25 +131,32 @@
             src_ref=src, dst_ref=dst, send_sem=ssem.at[j, k], recv_sem=rsem.at[j, k], **to
         )
 
-    def part(d, src, dst, lead, depth, own_x, cut=None):
+    def part(d, src, dst, lead, depth, own_x, cut=None, rows=None):
         xs, ys = src_span(d[0], NX, 1, depth[0]), src_span(d[1], NY, 1, depth[1])
         xd = dst_span(d[0], NX, own_x, 1, depth[0])
         yd = dst_span(d[1], NY, Y0, 1, depth[1])
         if cut:
             xs, xd = pl.ds(cut[0], cut[1]), pl.ds(own_x + cut[0], cut[1])
+        if rows:
+            ys, yd = pl.ds(rows[0], rows[1]), pl.ds(Y0 + rows[0], rows[1])
         return src.at[lead + (xs, ys)], dst.at[lead + (xd, yd)]
 
-    def state_parts(d, cut):
-        parts = [part(d, pop, s0, (pl.ds(a, n),), depth, X0, cut) for a, n, depth in runs_of(*d)]
-        parts.append(part(d, vel, u0, (pl.ds(0, 3),), (2, 2), X0, cut))
-        parts.append(part(d, obj, obj0, (), (2, 2), X0, cut))
-        parts.append(part(d, liq, liq0, (), (2, 2), X0, cut))
+    def state_parts(d, *cuts):
+        parts = [part(d, pop, s0, (pl.ds(a, n),), depth, X0, *cuts) for a, n, depth in runs_of(*d)]
+        parts.append(part(d, vel, u0, (pl.ds(0, 3),), (2, 2), X0, *cuts))
+        parts.append(part(d, obj, obj0, (), (2, 2), X0, *cuts))
+        parts.append(part(d, liq, liq0, (), (2, 2), X0, *cuts))
         return parts
 
     even = grp % 2 == 0
 
     def rim_parts(d):
-        return state_parts(d, None if d[0] else (jnp.where(even, 0, 3), NX - 3))
+        if not d[0]:
+            return state_parts(d, (jnp.where(even, 0, 3), NX - 3))
+        return state_parts(d, None, None if d[1] else (0, LOW_ROWS))
+
+    def upper_parts(d):
+        return state_parts(d, None, (LOW_ROWS, NY - LOW_ROWS))
 
     def near_parts(d):
         return state_parts(d, (jnp.where(even, NX - 3, 0), 3))
@@ -202,8 +210,8 @@
             for xs, ys, xd, yd in pieces
         ]
 
-    RIM, SPAN, SENS, NEAR, PASSED = range(5)
-    stages = (rim_parts, span_parts, sens_parts, near_parts, passed_parts)
+    RIM, SPAN, SENS, NEAR, PASSED, UPPER = range(6)
+    stages = (rim_parts, span_parts, sens_parts, near_parts, passed_parts, upper_parts)
 
     def whole(j, d):
         rows = count.at[pl.ds(0, rows_in(*(src for src, _ in stages[j](d))))]
@@ -229,6 +237,8 @@
     def directions(j):
         if j == NEAR:
             return ((0, 1), (0, -1))
+        if j == UPPER:
+            return ((1, 0), (-1, 0))
         if j == PASSED:
             return ((1, 1), (1, -1), (-1, 1), (-1, -1))
         return DIRS
@@ -251,8 +261,9 @@
 
     corners = ((1, 1), (1, -1), (-1, 1), (-1, -1))
     order = corners + ((1, 0), (-1, 0), (0, 1), (0, -1))
-    work = [(RIM, d) for d in order[4:6] + corners] + [(NEAR, (0, 1)), (NEAR, (0, -1))]
-    work += [(RIM, d) for d in order[6:]]
+    work = [(RIM, d) for d in ((1, 1), (-1, 1), (1, 0), (-1, 0))] + [(NEAR, (0, 1)), (NEAR, (0, -1))]
+    work += [(UPPER, (1, 0)), (UPPER, (-1, 0)), (RIM, (1, -1)), (RIM, (-1, -1))]
+    work += [(RIM, (0, 1)), (RIM, (0, -1))]
 
     def greet(d):
         pl.semaphore_signal(ready.at[DIRS.index(d)], inc=1, **peer(d))
@@ -399,9 +410,9 @@
 
     for side in (1, -1):
         low = side > 0
-        for j in (RIM, PASSED):
+        for j in (RIM, PASSED, UPPER):
             for d in directions(j):
-                if d[1] == side or (low and d[1] == 0):
+                if d[1] == side or (d[1] == 0 and low == (j == RIM)):
                     pl.when(gets(j, d))(lambda j=j, d=d: whole(j, d).wait_recv())
         starts = ((Y0 - 2, Y0 + 2), (Y0 - 1, Y0 + 1), (Y0,)) if low else ((Y0 + 10,), (Y0 + 9,), (Y0 + 8,))
         planes(1, STEP_X - 1, 4 if low else 6, functools.partial(step_1, starts[0]))
@@ -428,7 +439,7 @@
     planes(0, FILTER_X, 4, weigh)
 
     wait_recv(SENS)
-    for j in (RIM, SPAN, SENS, NEAR):
+    for j in (RIM, SPAN, SENS, NEAR, UPPER):
         wait_send(j)
 
 
@@ -504,8 +515,8 @@
             pltpu.VMEM((2,) + step_frame, f32),
             pltpu.VMEM((1024, NZ), f32),
             pltpu.SemaphoreType.DMA((6,)),
-            pltpu.SemaphoreType.DMA((5, 8)),
-            pltpu.SemaphoreType.DMA((5, 8)),
+            pltpu.SemaphoreType.DMA((6, 8)),
+            pltpu.SemaphoreType.DMA((6, 8)),
             pltpu.SemaphoreType.REGULAR((8,)),
         ],
         compiler_params=pltpu.CompilerParams(

time: 24.2 us -> 22.7 us (0.938)
  Pallas kernels: 23.4 us -> 22 us
    pallas_call x1, Pallas kernels: 21.8 us -> 20.3 us  [on_device(): pl.pallas_call(exchange_kernel, out_shape=(jax.ShapeDtypeStruct((19, NX,...]
where the time goes in v3:
time: 22.7 us; the launch traced here: 22.6 us
  Pallas kernels  22 us (97%)
  between operations  0.64 us (3%)
    pallas_call x1, Pallas kernels, on_device(): pl.pallas_call(exchange_kernel, out_shape=(jax.ShapeDtypeStruct((19, NX,...  20.3 us
    pallas_call x1, Pallas kernels, on_device(): pl.pallas_call(sweep_kernel, out_shape=(jax.ShapeDtypeStruct((19, NX, NY,...  1.66 us

profile of v3, /device:TPU:102, one launch (start us, length us, event | category | flops | bytes accessed | tf_op | source)
XLA Modules:
  0.0 22.6 jit_solution(12893180578550815650)
XLA Ops:
  0.6 20.3 %steps.1 = (f32[19,8,16,128]{3,2,1,0:T(8,128)S(1)}, f32[24,48,128]{2,1,0:T(8,128)S(1)}, f32[24,48,128]{2,1,0:T(8,128)S(1)}, f32[24,48,128]{2,1,0:T(8,128)S(1)}) custom-call(f32[19,8,16,128]{3,2,1,0:T(8,128)} %pop.1, f32[3,8,16,128]{3,2,1,0:T(8,128)} %vel.1, f32[8,16,128]{2,1,0:T(8,128)} %heat.1, f32[8,16,128]{2,1,0:T(8,128)} %obj.1, s32[8,16,128]{2,1,0:T(8,128)} %liq.1, ...), custom_call_target="tpu_custom_call" | custom-call | tf_op jit(solution)/shard_map/steps/pallas_call | solution.py:494
  21.0 1.7 %sweeps.1 = (f32[19,8,16,128]{3,2,1,0:T(8,128)}, f32[8,16,128]{2,1,0:T(8,128)}) custom-call(f32[19,8,16,128]{3,2,1,0:T(8,128)S(1)} %get-tuple-element.6.state, f32[24,48,128]{2,1,0:T(8,128)S(1)} %get-tuple-element.7.sens, f32[24,48,128]{2,1,0:T(8,128)S(1)} %get-tuple-element.8.scale, f32[24,48,128]{2,1,0:T(8,128)S(1)} %get-tuple-element.9.gain), custom_call_target="tpu_custom_call" | custom-call | tf_op jit(solution)/shard_map/sweeps/pallas_call | solution.py:527

commit v4 on v3

--- a/solution.py
+++ b/solution.py
@@ -410,17 +410,22 @@
 
     for side in (1, -1):
         low = side > 0
-        for j in (RIM, PASSED, UPPER):
-            for d in directions(j):
-                if d[1] == side or (d[1] == 0 and low == (j == RIM)):
-                    pl.when(gets(j, d))(lambda j=j, d=d: whole(j, d).wait_recv())
         starts = ((Y0 - 2, Y0 + 2), (Y0 - 1, Y0 + 1), (Y0,)) if low else ((Y0 + 10,), (Y0 + 9,), (Y0 + 8,))
-        planes(1, STEP_X - 1, 4 if low else 6, functools.partial(step_1, starts[0]))
+        one, two, three = (functools.partial(f, r) for f, r in zip((step_1, step_2, step_3), starts))
+        pl.when(gets(RIM, (0, side)))(lambda: whole(RIM, (0, side)).wait_recv())
         for d in corners:
             if d[1] == side:
                 pl.when(sends(PASSED, d))(lambda d=d: whole(PASSED, d).wait_send())
-        planes(2, STEP_X - 2, 5, functools.partial(step_2, starts[1]))
-        planes(3, STEP_X - 3, 8, functools.partial(step_3, starts[2]))
+        planes(X0 + 1, X0 + NX - 1, 3 if low else 6, one)
+        planes(X0 + 2, X0 + NX - 2, 4, two)
+        planes(X0 + 3, X0 + NX - 3, 2, three)
+        for j in (RIM, PASSED, UPPER):
+            for d in directions(j):
+                if d[0] and (d[1] == side or (d[1] == 0 and low == (j == RIM))):
+                    pl.when(gets(j, d))(lambda j=j, d=d: whole(j, d).wait_recv())
+        for n, body in ((1, one), (2, two), (3, three)):
+            planes(n, X0 + n, 3, body)
+            planes(X0 + NX - n, STEP_X - n, 3, body)
         for d in order:
             if d[1] in (0, -side):
                 pl.when(exists(d))(lambda d=d: send(SENS, d, 0 if low else 1))

time: 22.7 us -> 22.7 us (level)
  the two profiles are of different devices: /device:TPU:102 before, /device:TPU:251 now
where the time goes in v4:
time: 22.7 us; the launch traced here: 22.6 us
  Pallas kernels  22 us (97%)
  between operations  0.64 us (3%)
    pallas_call x1, Pallas kernels, on_device(): pl.pallas_call(exchange_kernel, out_shape=(jax.ShapeDtypeStruct((19, NX,...  20.3 us
    pallas_call x1, Pallas kernels, on_device(): pl.pallas_call(sweep_kernel, out_shape=(jax.ShapeDtypeStruct((19, NX, NY,...  1.66 us

profile of v4, /device:TPU:251, one launch (start us, length us, event | category | flops | bytes accessed | tf_op | source)
XLA Modules:
  0.0 22.6 jit_solution(10147943191775367707)
XLA Ops:
  0.6 20.3 %steps.1 = (f32[19,8,16,128]{3,2,1,0:T(8,128)S(1)}, f32[24,48,128]{2,1,0:T(8,128)S(1)}, f32[24,48,128]{2,1,0:T(8,128)S(1)}, f32[24,48,128]{2,1,0:T(8,128)S(1)}) custom-call(f32[19,8,16,128]{3,2,1,0:T(8,128)} %pop.1, f32[3,8,16,128]{3,2,1,0:T(8,128)} %vel.1, f32[8,16,128]{2,1,0:T(8,128)} %heat.1, f32[8,16,128]{2,1,0:T(8,128)} %obj.1, s32[8,16,128]{2,1,0:T(8,128)} %liq.1, ...), custom_call_target="tpu_custom_call" | custom-call | tf_op jit(solution)/shard_map/steps/pallas_call | solution.py:499
  20.9 1.7 %sweeps.1 = (f32[19,8,16,128]{3,2,1,0:T(8,128)}, f32[8,16,128]{2,1,0:T(8,128)}) custom-call(f32[19,8,16,128]{3,2,1,0:T(8,128)S(1)} %get-tuple-element.6.state, f32[24,48,128]{2,1,0:T(8,128)S(1)} %get-tuple-element.7.sens, f32[24,48,128]{2,1,0:T(8,128)S(1)} %get-tuple-element.8.scale, f32[24,48,128]{2,1,0:T(8,128)S(1)} %get-tuple-element.9.gain), custom_call_target="tpu_custom_call" | custom-call | tf_op jit(solution)/shard_map/sweeps/pallas_call | solution.py:532
